TPU v7x, 128 devices: a whole 4x4x4 slice. The times are simulated.
128 devices in a mesh: seq: 32 (over y, x_hi, z), chan: 4 (over x_lo, core).
Axes of the slice: x: 4 (x_hi: 2, x_lo: 2; x = x_hi * 2 + x_lo), y: 4, z: 4, core: 2. Of those that a mesh axis runs over, the one named last changes fastest.
Arguments:
- inputs: bfloat16 [256, 512, 1536], P('seq', None, 'chan'), may hold values from -6 to 6
- gate_values: bfloat16 [256, 512, 1536], P('seq', None, 'chan'), may hold values from -6 to 6
- kernel: bfloat16 [256, 512, 1536], P('seq', None, 'chan'), may hold values from -6 to 6
- grad_out: bfloat16 [512, 256, 1536], P('seq', None, 'chan'), may hold values from -6 to 6
- left_tiles: bfloat16 [256, 8, 256], P(('seq', 'chan')), may hold values from -0.375 to 0.375
- right_tiles: bfloat16 [512, 8, 512], P(('seq', 'chan')), may hold values from -0.25 to 0.25
Outputs:
- output: bfloat16 [512, 256, 1536], P('seq', None, 'chan')
- grad_inputs: bfloat16 [256, 512, 1536], P('seq', None, 'chan')
- grad_gates: bfloat16 [256, 512, 1536], P('seq', None, 'chan')
- grad_kernel: bfloat16 [256, 512, 1536], P('seq', None, 'chan')
- grad_left: float32 [256, 8, 256], P(('seq', 'chan'))
- grad_right: float32 [512, 8, 512], P(('seq', 'chan'))
All inputs are finite; a program needn't handle non-finite values.
Results may differ from a plain program's by a relative error of at most 0.0058.
Values may be sent and summed in bfloat16 or wider, within the bound.
A program may use at most 192 MiB of HBM per device.

v0:
```python
import math

import jax
import jax.numpy as jnp
from jax import lax
from jax.sharding import PartitionSpec as P

A = 256
B = 512
C = 1536
H = 8


def on_device(inputs, gate_values, kernel, grad_out, left_tiles, right_tiles):
    groups = right_tiles.shape[1]
    row_count = inputs.shape[0]
    span_b = inputs.shape[1]
    chans = inputs.shape[2]
    depth = chans // groups
    col_count = grad_out.shape[0]
    span_a = grad_out.shape[1]
    gated = (inputs.astype(jnp.float32) * gate_values.astype(jnp.float32)).astype(jnp.bfloat16)
    gated_four = gated.reshape(row_count, span_b, depth, groups)
    kernel_four = kernel.astype(jnp.float32).reshape(row_count, span_b, depth, groups)
    spectral = jnp.einsum(
        "phb,abdh->apdh",
        lax.all_gather(right_tiles, ("seq", "chan"), axis=0, tiled=True),
        gated_four,
        preferred_element_type=jnp.float32,
    )
    twisted = (kernel_four * spectral).astype(jnp.bfloat16)
    turned = lax.all_to_all(twisted, "seq", split_axis=1, concat_axis=0, tiled=True)
    mixed = jnp.einsum(
        "qha,apdh->pqdh",
        lax.all_gather(left_tiles, ("seq", "chan"), axis=0, tiled=True),
        turned,
        preferred_element_type=jnp.float32,
    )
    output = mixed.astype(jnp.bfloat16).reshape(col_count, span_a, chans)
    cotangent = grad_out.reshape(col_count, span_a, depth, groups)
    block = cotangent
    back_turned = jnp.einsum(
        "qha,pqdh->apdh",
        lax.all_gather(left_tiles, ("seq", "chan"), axis=0, tiled=True),
        block,
        preferred_element_type=jnp.float32,
    )
    block = cotangent
    left_sum = lax.psum_scatter(
        jnp.einsum("pqdh,apdh->qha", block, turned, preferred_element_type=jnp.float32),
        ("seq", "chan"),
        scatter_dimension=0,
        tiled=True,
    )
    grad_left = left_sum / math.sqrt(B * C / H)
    back_local = lax.all_to_all(
        back_turned.astype(jnp.bfloat16), "seq", split_axis=0, concat_axis=1, tiled=True
    )
    back_float = back_local.astype(jnp.float32)
    grad_kernel = (back_float * spectral).astype(jnp.bfloat16).reshape(row_count, span_b, chans)
    pushed = (kernel_four * back_float).astype(jnp.bfloat16)
    block = pushed
    grad_gated = jnp.einsum(
        "phb,apdh->abdh",
        lax.all_gather(right_tiles, ("seq", "chan"), axis=0, tiled=True),
        block,
        preferred_element_type=jnp.float32,
    )
    grad_gated = grad_gated.reshape(row_count, span_b, chans)
    grad_inputs = (grad_gated * gate_values.astype(jnp.float32)).astype(jnp.bfloat16)
    grad_gates = (grad_gated * inputs.astype(jnp.float32)).astype(jnp.bfloat16)
    block = pushed
    right_sum = lax.psum_scatter(
        jnp.einsum("apdh,abdh->phb", block, gated_four, preferred_element_type=jnp.float32),
        ("seq", "chan"),
        scatter_dimension=0,
        tiled=True,
    )
    grad_right = right_sum / math.sqrt(A * C / H)
    return (output, grad_inputs, grad_gates, grad_kernel, grad_left, grad_right)


def solution(mesh):
    in_specs = (
        P("seq", None, "chan"),
        P("seq", None, "chan"),
        P("seq", None, "chan"),
        P("seq", None, "chan"),
        P(("seq", "chan"), None, None),
        P(("seq", "chan"), None, None),
    )
    out_specs = (
        P("seq", None, "chan"),
        P("seq", None, "chan"),
        P("seq", None, "chan"),
        P("seq", None, "chan"),
        P(("seq", "chan"), None, None),
        P(("seq", "chan"), None, None),
    )
    return jax.shard_map(
        on_device, mesh=mesh, in_specs=in_specs, out_specs=out_specs, check_vma=False
    )
```

profile of v0, /device:TPU:0, one launch (start us, length us, event | category | flops | bytes accessed | tf_op | source)
XLA Modules:
  0.0 1874.1 jit_solution(13961861417345871807)
XLA Ops:
  11.8 191.2 %all-gather.5.cloned.1.call-done = bf16[256,8,256]{2,1,0:T(8,128)(2,1)} async-done(((bf16[2,8,256]{2,1,0:T(8,128)(2,1)}), bf16[256,8,256]{2,1,0:T(8,128)(2,1)}) %all-gather.5.cloned.1.call-update) | async-done | bytes 1048592 | tf_op jit(solution)/shard_map/all_gather | solution.py:35
  206.9 12.6 copy.67
  219.5 18.5 reshape.56
  261.0 25.7 %all-to-all-done.1 = bf16[32,2,24576]{2,1,0:T(2,128)(2,1)} async-done(((bf16[32,2,24576]{2,1,0:T(2,128)(2,1)}), bf16[32,2,24576]{2,1,0:T(2,128)(2,1)}, u32[]{:S(2)}, u32[]{:S(2)}) %all-to-all-start.1) | async-done | bytes 3145760 | tf_op jit(solution)/shard_map/all_to_all | solution.py:56
  286.7 13.2 reshape.57
  299.9 10.9 copy.68
  310.8 11.2 convert_bitcast_fusion
  322.0 11.7 copy.69
  333.8 12.9 copy.70
  346.6 12.3 copy.74
  364.5 69.9 %all-gather.3.cloned.1.call-done = bf16[512,8,512]{2,1,0:T(8,128)(2,1)} async-done(((bf16[4,8,512]{2,1,0:T(8,128)(2,1)}), bf16[512,8,512]{2,1,0:T(8,128)(2,1)}) %all-gather.3.cloned.1.call-update) | async-done | bytes 4194320 | tf_op jit(solution)/shard_map/all_gather | solution.py:27
  434.4 7.4 fusion.18
  441.8 7.3 fusion
  449.2 14.6 fusion.4
  463.8 12.6 copy.58
  476.4 18.4 reshape.54
  494.9 46.7 %all_to_all.27 = bf16[32,2,24576]{2,1,0:T(2,128)(2,1)} all-to-all(bf16[32,2,24576]{2,1,0:T(2,128)(2,1)} %reshape.54), channel_id=1, replica_groups=mesh['seq'=32,'chan'=4] {'seq'}, dimensions={0} | all-to-all | bytes 6291456 | tf_op jit(solution)/shard_map/all_to_all | solution.py:32
  541.6 13.2 reshape.55
  554.7 9.2 copy.60
  563.9 10.4 copy.61
  583.1 11.0 convolution_bitcast_fusion
  594.1 10.5 copy.81
  627.3 592.4 %reduce-scatter.3.cloned.1.call-done = f32[2,8,256]{2,1,0:T(8,128)} async-done(((f32[256,8,256]{2,1,0:T(8,128)}), f32[2,8,256]{2,1,0:T(8,128)}) %reduce-scatter.3.cloned.1.call-update) | async-done | bytes 16400 | tf_op jit(solution)/shard_map/reduce_scatter | solution.py:49
  1221.0 644.9 %reduce-scatter.5.cloned.1.call-done = f32[4,8,512]{2,1,0:T(8,128)} async-done(((f32[512,8,512]{2,1,0:T(8,128)}), f32[4,8,512]{2,1,0:T(8,128)}) %reduce-scatter.5.cloned.1.call-update) | async-done | bytes 65552 | tf_op jit(solution)/shard_map/reduce_scatter | solution.py:73
  (42 shorter events, 71.4 us)
Async XLA Ops:
  7.2 195.9 %all-gather.5.cloned.1.call-start = ((), (), s32[]{:S(2)}) async-start(), calls=%async_computation.5 | async-start | bytes 1056768 | tf_op jit(solution)/shard_map/all_gather | solution.py:35
  7.9 426.5 %all-gather.3.cloned.1.call-start = ((), (), s32[]{:S(2)}) async-start(), calls=%async_computation.4 | async-start | bytes 4227072 | tf_op jit(solution)/shard_map/all_gather | solution.py:27
  11.8 195.1 %copy-start.4 = (bf16[16,256,384]{1,2,0:T(8,128)(2,1)}, bf16[16,256,384]{1,2,0:T(8,128)(2,1)S(1)}, u32[]{:S(2)}) copy-start(bf16[16,256,384]{1,2,0:T(8,128)(2,1)S(1)} %copy.64) | copy-start | bytes 9437188
  237.9 48.8 %all-to-all-start.1 = ((bf16[32,2,24576]{2,1,0:T(2,128)(2,1)}), bf16[32,2,24576]{2,1,0:T(2,128)(2,1)}, u32[]{:S(2)}, u32[]{:S(2)}) async-start(bf16[32,2,24576]{2,1,0:T(2,128)(2,1)} %reshape.56), calls=%async_computation.1 | async-start | bytes 6291456 | tf_op jit(solution)/shard_map/all_to_all | solution.py:56
  244.8 974.9 %reduce-scatter.3.cloned.1.call-start = ((), (), s32[]{:S(2)}) async-start(), calls=%async_computation.6 | async-start | bytes 2113536 | tf_op jit(solution)/shard_map/reduce_scatter | solution.py:49
  434.4 7.4 copy-start.2
  434.4 7.4 copy-start.3
  434.4 14.8 slice-start
  441.8 7.4 slice-start.1
  583.1 1282.9 %reduce-scatter.5.cloned.1.call-start = ((), (), s32[]{:S(2)}) async-start(), calls=%async_computation.7 | async-start | bytes 8454144 | tf_op jit(solution)/shard_map/reduce_scatter | solution.py:73
  608.1 4.8 copy-start.1
  615.7 4.8 copy-start
Sparse Core Ops, SparseCore 0:
  9.7 193.2 all-gather.4
  204.7 229.6 all-gather.2
  583.2 636.4 reduce-scatter.2
  1222.0 643.8 reduce-scatter.4
where the time goes:
time: 1880 us; the launch traced here: 1870 us
  waiting for transfers between devices  1530 us (81%)
  local copies, waits for them, and re-layouts  205 us (11%)
  blocking collectives  46.7 us (2%)
  matrix products  44.8 us (2%)
  other arithmetic  30.4 us (2%)
    reduce_scatter x1, waiting for transfers between devices, on_device(): lax.psum_scatter(jnp.einsum('apdh,abdh->phb', block, gated_four, preferre...  645 us
    reduce_scatter x1, waiting for transfers between devices, on_device(): lax.psum_scatter(jnp.einsum('pqdh,apdh->qha', block, turned, preferred_el...  592 us
    all_gather x1, waiting for transfers between devices, on_device(): lax.all_gather(left_tiles, ('seq', 'chan'), axis=0, tiled=True)  191 us
    unnamed x26, local copies, waits for them, and re-layouts  94 us
    all_gather x1, waiting for transfers between devices, on_device(): lax.all_gather(right_tiles, ('seq', 'chan'), axis=0, tiled=True)  69.9 us
    all_to_all x1, blocking collectives, on_device(): lax.all_to_all(twisted, 'seq', split_axis=1, concat_axis=0, tiled=True)  46.7 us
  transfers between devices with their start and end apart: 5, of which 5 were waited for; matrix products, arithmetic and copies ran while one was open for 9% of the time, Pallas kernels for 0%

commit v1 on v0

v1 whole, which is shorter than its diff:
```python
import functools
import math

import jax
import jax.numpy as jnp
from jax import lax
from jax.experimental import pallas as pl
from jax.experimental.pallas import tpu as pltpu
from jax.sharding import PartitionSpec as P

MESH = pl.DeviceIdType.MESH
BF = jnp.bfloat16
F32 = jnp.float32
A = 256
B = 512
C = 1536
H = 8
LANE = 128
SEQ = 32
RIGHT_PARTS = ((0, 32, (0, 1, 2)), (32, 16, (1, 2, 0)), (48, 16, (2, 0, 1)))
LEFT_PARTS = ((0, 32, (2, 0, 1)),)


def place():
    seq = lax.axis_index("seq")
    chan = lax.axis_index("chan")
    x = ((seq // 4) % 2) * 2 + chan // 2
    return (x, seq // 8, seq % 4), chan % 2


def device_at(xyz, core):
    x, y, z = xyz
    return (y * 8 + (x // 2) * 4 + z, (x % 2) * 2 + core)


def moved(xyz, axis, step):
    new = list(xyz)
    new[axis] = (xyz[axis] + step) % 4
    return tuple(new)


def greet(devices):
    barrier = pltpu.get_barrier_semaphore()
    for device in devices:
        pl.semaphore_signal(barrier, inc=1, device_id=device, device_id_type=MESH)
    pl.semaphore_wait(barrier, len(devices))


def chip_friends(xyz, core):
    return [device_at(xyz, 1 - core)] + [
        device_at(moved(xyz, axis, step), core) for axis in range(3) for step in (1, 2, 3)
    ]


def remote(src, dst, send, recv, device):
    return pltpu.make_async_remote_copy(
        src_ref=src, dst_ref=dst, send_sem=send, recv_sem=recv, device_id=device, device_id_type=MESH
    )


def aligned(value, multiple):
    return pl.multiple_of(value, multiple)


def gather_kernel(right_ref, left_ref, right_out, left_out, raw_r, raw_l, piece, local_sem, core_sems, axis_sems):
    xyz, core = place()
    x, y, z = xyz
    sibling = device_at(xyz, 1 - core)
    greet(chip_friends(xyz, core))
    half_r = pl.ds(aligned(core * 256, 256), 256)
    half_l = pl.ds(aligned(core * 128, 128), 128)
    other_r = pl.ds(aligned((1 - core) * 256, 256), 256)
    other_l = pl.ds(aligned((1 - core) * 128, 128), 128)
    rows_r = pl.ds(aligned(core * 32, 32), 32)
    rows_l = pl.ds(aligned(core * 16, 16), 16)
    first = [
        remote(right_ref.at[:, other_r], raw_r.at[x, y, z, rows_r, other_r], core_sems.at[0, 0], core_sems.at[1, 0], sibling),
        remote(left_ref.at[:, other_l], raw_l.at[x, y, z, rows_l, other_l], core_sems.at[0, 1], core_sems.at[1, 1], sibling),
    ]
    for copy in first:
        copy.start()
    own = [
        pltpu.make_async_copy(right_ref.at[:, half_r], raw_r.at[x, y, z, rows_r, half_r], local_sem.at[0]),
        pltpu.make_async_copy(left_ref.at[:, half_l], raw_l.at[x, y, z, rows_l, half_l], local_sem.at[1]),
    ]
    for copy in own:
        copy.start()
    for copy in own:
        copy.wait()
    for copy in first:
        copy.wait()
    parts = [(raw_l, half_l) + part for part in LEFT_PARTS] + [(raw_r, half_r) + part for part in RIGHT_PARTS]
    stages = {}
    for stage in range(4):
        for number, (buf, half, row, rows, order) in enumerate(parts):
            if stage > 0:
                for copy in stages[number]:
                    copy.wait()
            if stage == 3:
                continue
            index = tuple(slice(None) if axis in order[:stage] else xyz[axis] for axis in range(3))
            ref = buf.at[index + (pl.ds(row, rows), half)]
            stages[number] = [
                remote(
                    ref,
                    ref,
                    axis_sems.at[0, number, stage, step - 1],
                    axis_sems.at[1, number, stage, step - 1],
                    device_at(moved(xyz, order[stage], step), core),
                )
                for step in (1, 2, 3)
            ]
            for copy in stages[number]:
                copy.start()
    mine = [raw_l.at[:, :, :, :, half_l], raw_r.at[:, :, :, :, half_r]]
    last = [
        remote(ref, ref, core_sems.at[0, 2 + n], core_sems.at[1, 2 + n], sibling) for n, ref in enumerate(mine)
    ]
    for copy in last:
        copy.start()
    for copy in last:
        copy.wait()

    def right_rows(seq, _):
        cy, cx, cz = seq // 8, (seq // 4) % 2, seq % 4
        for lane in range(4):
            lanes = slice(lane * LANE, (lane + 1) * LANE)
            for lo in range(2):
                piece[lane, lo * 64 : lo * 64 + 64, :] = raw_r[cx * 2 + lo, cy, cz, :, lanes].astype(F32)
            for h in range(H):
                right_out[h, pl.ds(aligned(seq * 16, 16), 16), lanes] = piece[lane, pl.ds(h, 16, stride=8), :].astype(BF)
        return _

    def left_rows(pair, _):
        seq = pair * 2
        cy, cx, cz = seq // 8, (seq // 4) % 2, seq % 4
        for lane in range(2):
            lanes = slice(lane * LANE, (lane + 1) * LANE)
            for n in range(4):
                piece[lane, n * 32 : n * 32 + 32, :] = raw_l[cx * 2 + n % 2, cy, cz + n // 2, :, lanes].astype(F32)
            for h in range(H):
                left_out[h, pl.ds(aligned(pair * 16, 16), 16), lanes] = piece[lane, pl.ds(h, 16, stride=8), :].astype(BF)
        return _

    lax.fori_loop(0, 16, left_rows, 0)
    lax.fori_loop(0, 32, right_rows, 0)


def gather_tiles(right, left):
    vmem = pl.BlockSpec(memory_space=pltpu.VMEM)
    return pl.pallas_call(
        gather_kernel,
        out_shape=(jax.ShapeDtypeStruct((H, B, B), BF), jax.ShapeDtypeStruct((H, A, A), BF)),
        in_specs=[vmem, vmem],
        out_specs=(vmem, vmem),
        scratch_shapes=[
            pltpu.VMEM((4, 4, 4, 64, 512), BF),
            pltpu.VMEM((4, 4, 4, 32, 256), BF),
            pltpu.VMEM((4, 128, LANE), F32),
            pltpu.SemaphoreType.DMA((2,)),
            pltpu.SemaphoreType.DMA((2, 4)),
            pltpu.SemaphoreType.DMA((2, 4, 3, 3)),
        ],
        compiler_params=pltpu.CompilerParams(collective_id=0, has_side_effects=True, vmem_limit_bytes=40 << 20),
        name="gather_tiles",
    )(right, left)


def masks_of(rows):
    lane = lax.broadcasted_iota(jnp.int32, (rows, LANE), 1)
    return [(lane & bit) != 0 for bit in (1, 2, 4)]


def turn(values, masks):
    for bit, mask in zip((1, 2, 4), masks):
        values = [jnp.where(mask, values[(i + bit) % 8], values[i]) for i in range(8)]
    return values


def to_groups(values, masks):
    values = turn([v if n == 0 else pltpu.roll(v, n, 1) for n, v in enumerate(values)], masks)
    return [values[(-h) % 8] for h in range(8)]


def from_groups(values, masks):
    values = turn(values, masks)
    return [values[0]] + [pltpu.roll(values[(-n) % 8], LANE - n, 1) for n in range(1, 8)]


def dot(a, b, ca, cb):
    return lax.dot_general(a, b, (((ca,), (cb,)), ((), ())), preferred_element_type=F32)


def seq_offset(k):
    return (k * 11) % SEQ


def seq_moved(seq, off, sign):
    y, xh, z = seq // 8, (seq // 4) % 2, seq % 4
    dy, dx, dz = off // 8, (off // 4) % 2, off % 4
    return ((y + sign * dy + 4) % 4) * 8 + ((xh + dx) % 2) * 4 + (z + sign * dz + 4) % 4


def exchange_copy(k, src, dst, send, recv):
    me = lax.axis_index("seq")
    peer = seq_moved(me, seq_offset(k), 1)
    return remote(
        src.at[:, pl.ds(aligned(peer * 16, 16), 16), :],
        dst.at[:, pl.ds(aligned(me * 16, 16), 16), :],
        send.at[k],
        recv.at[k],
        (peer, lax.axis_index("chan")),
    )


def exchange_start(src, dst, send, recv, local):
    me = lax.axis_index("seq")
    rows = pl.ds(aligned(me * 16, 16), 16)

    def step(k, _):
        exchange_copy(k, src, dst, send, recv).start()
        return _

    lax.fori_loop(1, SEQ, step, 0)
    copy = pltpu.make_async_copy(src.at[:, rows, :], dst.at[:, rows, :], local)
    copy.start()
    return copy


def exchange_recv(src, dst, send, recv, own):
    own.wait()

    def step(k, _):
        exchange_copy(k, src, dst, send, recv).wait_recv()
        return _

    lax.fori_loop(1, SEQ, step, 0)


def exchange_sent(src, dst, send, recv):
    def step(k, _):
        exchange_copy(k, src, dst, send, recv).wait_send()
        return _

    lax.fori_loop(1, SEQ, step, 0)


def blocks(body):
    def step(i, _):
        row = aligned(i * 16, 16)
        for j in range(3):
            body(i, row, slice(j * LANE, (j + 1) * LANE))
        return _

    lax.fori_loop(0, 32, step, 0)


def main_kernel(
    in_ref, gate_ref, ker_ref, cot_ref, right_ref, left_ref,
    out_ref, gin_ref, ggate_ref, gker_ref, gleft_ref, gright_ref,
    xin, xgate, xker, cot, gated, bsend, brecv, tsend, trecv, tgrp, right, left, work, piece, stage,
    load, own, sems, stores, stage_sems,
):
    me = lax.axis_index("seq")
    chan = lax.axis_index("chan")
    barrier = pltpu.get_barrier_semaphore()

    def hello(k, _):
        pl.semaphore_signal(barrier, inc=1, device_id=(seq_moved(me, seq_offset(k), 1), chan), device_id_type=MESH)
        return _

    loads = {
        "cot0": pltpu.make_async_copy(cot_ref.at[pl.ds(0, 8)], cot.at[:, pl.ds(0, 256), :], load.at[0]),
        "cot1": pltpu.make_async_copy(cot_ref.at[pl.ds(8, 8)], cot.at[:, pl.ds(256, 256), :], load.at[1]),
        "left": pltpu.make_async_copy(left_ref, left, load.at[2]),
        "in": pltpu.make_async_copy(in_ref, xin, load.at[3]),
        "gate": pltpu.make_async_copy(gate_ref, xgate, load.at[4]),
        "right": pltpu.make_async_copy(right_ref, right, load.at[5]),
        "ker": pltpu.make_async_copy(ker_ref, xker, load.at[6]),
    }
    for copy in loads.values():
        copy.start()
    lax.fori_loop(1, SEQ, hello, 0)
    pl.semaphore_wait(barrier, SEQ - 1)
    masks = masks_of(16)

    loads["cot0"].wait()
    loads["cot1"].wait()

    def cot_groups(i, row, lanes):
        values = [cot[n, pl.ds(row, 16), lanes].astype(F32) for n in range(8)]
        for h, value in enumerate(to_groups(values, masks)):
            cot[h, pl.ds(row, 16), lanes] = value.astype(BF)

    blocks(cot_groups)
    loads["left"].wait()

    def back_dot(h, _):
        for half in range(2):
            rows = slice(half * 256, half * 256 + 256)
            work[h, rows, :] = dot(left[h], cot[h, rows, :], 0, 0)
        return _

    lax.fori_loop(0, H, back_dot, 0)

    def back_rows(i, _):
        for j in range(3):
            lanes = slice(j * LANE, (j + 1) * LANE)
            for half in range(2):
                row = aligned(half * 256 + i * 16, 16)
                values = from_groups([work[h, pl.ds(row, 16), lanes] for h in range(8)], masks)
                for n, value in enumerate(values):
                    piece[j, pl.ds(half * 8 + n, 16, stride=16), :] = value
            for k in range(16):
                to = aligned((2 * i + k // 8) * 16, 16)
                bsend[k % 8, pl.ds(to, 16), lanes] = piece[j, k * 16 : k * 16 + 16, :].astype(BF)
        return _

    lax.fori_loop(0, 16, back_rows, 0)
    back = (bsend, brecv, sems.at[0], sems.at[1])
    back_own = exchange_start(*back, own.at[0])

    loads["in"].wait()
    loads["gate"].wait()

    def gate_groups(i, row, lanes):
        rows = pl.ds(row, 16)
        values = [xin[n, rows, lanes].astype(F32) * xgate[n, rows, lanes].astype(F32) for n in range(8)]
        for h, value in enumerate(to_groups(values, masks)):
            gated[h, rows, lanes] = value.astype(BF)

    blocks(gate_groups)
    loads["right"].wait()

    def inner_dot(h, _):
        work[h] = dot(right[h], gated[h], 1, 0)
        return _

    lax.fori_loop(0, H, inner_dot, 0)
    loads["ker"].wait()

    def twist(i, row, lanes):
        rows = pl.ds(row, 16)
        values = from_groups([work[h, rows, lanes] for h in range(8)], masks)
        for n, value in enumerate(values):
            work[n, rows, lanes] = value
            tsend[n, rows, lanes] = (xker[n, rows, lanes].astype(F32) * value).astype(BF)

    blocks(twist)
    exchange_recv(*back, back_own)
    twisted = (tsend, trecv, sems.at[2], sems.at[3])
    twisted_own = exchange_start(*twisted, own.at[1])

    def push(i, row, lanes):
        rows = pl.ds(row, 16)
        values = []
        for n in range(8):
            value = brecv[n, rows, lanes].astype(F32)
            weight = xker[n, rows, lanes].astype(F32)
            xker[n, rows, lanes] = (value * work[n, rows, lanes]).astype(BF)
            values.append(weight * value)
        for h, value in enumerate(to_groups(values, masks)):
            brecv[h, rows, lanes] = value.astype(BF)

    blocks(push)
    save = [pltpu.make_async_copy(xker, gker_ref, stores.at[0])]
    save[0].start()

    def gated_dot(h, _):
        work[h] = dot(right[h], brecv[h], 0, 0)
        return _

    lax.fori_loop(0, H, gated_dot, 0)

    def gate_grads(i, row, lanes):
        rows = pl.ds(row, 16)
        values = from_groups([work[h, rows, lanes] for h in range(8)], masks)
        for n, value in enumerate(values):
            first = xin[n, rows, lanes].astype(F32)
            second = xgate[n, rows, lanes].astype(F32)
            xin[n, rows, lanes] = (value * second).astype(BF)
            xgate[n, rows, lanes] = (value * first).astype(BF)

    blocks(gate_grads)
    save.append(pltpu.make_async_copy(xin, gin_ref, stores.at[1]))
    save.append(pltpu.make_async_copy(xgate, ggate_ref, stores.at[2]))
    save[1].start()
    save[2].start()

    for h in range(H):
        copy = pltpu.make_async_copy(stage.at[h % 2], gright_ref.at[h], stage_sems.at[h % 2])
        if h >= 2:
            copy.wait()
        stage[h % 2] = dot(brecv[h], gated[h], 1, 1)
        copy.start()
    for slot in range(2):
        pltpu.make_async_copy(stage.at[slot], gright_ref.at[slot], stage_sems.at[slot]).wait()

    exchange_recv(*twisted, twisted_own)

    def twist_groups(i, _):
        for j in range(3):
            lanes = slice(j * LANE, (j + 1) * LANE)
            for k in range(16):
                at = aligned((2 * i + k // 8) * 16, 16)
                piece[j, k * 16 : k * 16 + 16, :] = trecv[k % 8, pl.ds(at, 16), lanes].astype(F32)
            for half in range(2):
                values = [piece[j, pl.ds(half * 8 + n, 16, stride=16), :] for n in range(8)]
                for h, value in enumerate(to_groups(values, masks)):
                    tgrp[h, pl.ds(aligned(half * 256 + i * 16, 16), 16), lanes] = value.astype(BF)
        return _

    lax.fori_loop(0, 16, twist_groups, 0)

    def outer_dot(h, _):
        for half in range(2):
            rows = slice(half * 256, half * 256 + 256)
            work[h, rows, :] = dot(left[h], tgrp[h, rows, :], 1, 0)
        return _

    lax.fori_loop(0, H, outer_dot, 0)

    def out_rows(i, row, lanes):
        rows = pl.ds(row, 16)
        values = from_groups([work[h, rows, lanes] for h in range(8)], masks)
        for n, value in enumerate(values):
            trecv[n, rows, lanes] = value.astype(BF)

    blocks(out_rows)
    save.append(pltpu.make_async_copy(trecv.at[:, pl.ds(0, 256), :], out_ref.at[pl.ds(0, 8)], stores.at[3]))
    save.append(pltpu.make_async_copy(trecv.at[:, pl.ds(256, 256), :], out_ref.at[pl.ds(8, 8)], stores.at[4]))
    save[3].start()
    save[4].start()
    for h in range(H):
        value = dot(cot[h, :256, :], tgrp[h, :256, :], 1, 1) + dot(cot[h, 256:, :], tgrp[h, 256:, :], 1, 1)
        copy = pltpu.make_async_copy(stage.at[h % 2, pl.ds(0, 256), pl.ds(0, 256)], gleft_ref.at[h], stage_sems.at[h % 2])
        if h >= 2:
            copy.wait()
        stage[h % 2, :256, :256] = value
        copy.start()
    for slot in range(2):
        pltpu.make_async_copy(stage.at[slot, pl.ds(0, 256), pl.ds(0, 256)], gleft_ref.at[slot], stage_sems.at[slot]).wait()
    exchange_sent(*back)
    exchange_sent(*twisted)
    for copy in save:
        copy.wait()


def mix(inputs, gate_values, kernel, grad_out, right, left):
    hbm = pl.BlockSpec(memory_space=pl.ANY)
    rows = pltpu.VMEM((8, B, 384), BF)
    return pl.pallas_call(
        main_kernel,
        out_shape=(
            jax.ShapeDtypeStruct((16, A, 384), BF),
            jax.ShapeDtypeStruct((8, B, 384), BF),
            jax.ShapeDtypeStruct((8, B, 384), BF),
            jax.ShapeDtypeStruct((8, B, 384), BF),
            jax.ShapeDtypeStruct((H, A, A), F32),
            jax.ShapeDtypeStruct((H, B, B), F32),
        ),
        in_specs=[hbm] * 6,
        out_specs=(hbm,) * 6,
        scratch_shapes=[rows] * 10
        + [
            pltpu.VMEM((H, B, B), BF),
            pltpu.VMEM((H, A, A), BF),
            pltpu.VMEM((8, B, 384), F32),
            pltpu.VMEM((3, 256, LANE), F32),
            pltpu.VMEM((2, B, B), F32),
            pltpu.SemaphoreType.DMA((7,)),
            pltpu.SemaphoreType.DMA((2,)),
            pltpu.SemaphoreType.DMA((4, SEQ)),
            pltpu.SemaphoreType.DMA((5,)),
            pltpu.SemaphoreType.DMA((2,)),
        ],
        compiler_params=pltpu.CompilerParams(collective_id=1, has_side_effects=True, vmem_limit_bytes=60 << 20),
        name="mix",
    )(inputs, gate_values, kernel, grad_out, right, left)


def reduce_kernel(
    gright_ref, gleft_ref, right_out, left_out,
    own_r, own_l, sib_r, sib_l, got_r, got_l, d0_r, d1_r, d2_r, d0_l, d1_l, d2_l, full_r, full_l, piece,
    core_sems, axis_sems,
):
    xyz, core = place()
    sibling = device_at(xyz, 1 - core)
    greet(chip_friends(xyz, core))
    half_r = pl.ds(aligned(core * 256, 256), 256)
    half_l = pl.ds(aligned(core * 128, 128), 128)
    other_r = pl.ds(aligned((1 - core) * 256, 256), 256)
    other_l = pl.ds(aligned((1 - core) * 128, 128), 128)

    def left_piece(seq, lanes):
        for h in range(H):
            value = gleft_ref[h, pl.ds(aligned(seq * 8, 8), 8), lanes]
            piece[h * 4 : h * 4 + 4, :] = value[:4]
            piece[32 + h * 4 : 32 + h * 4 + 4, :] = value[4:]

    def pack_left(seq, _):
        cy, cx, cz = seq // 8, (seq // 4) % 2, seq % 4
        left_piece(seq, other_l)
        for lo in range(2):
            sib_l[cx * 2 + lo, cy, cz] = piece[lo * 32 : lo * 32 + 32, :].astype(BF)
        return _

    def right_tile(seq, lo, g, lanes):
        rows = pl.ds(aligned(seq * 16 + lo * 8, 8), 8)
        return jnp.concatenate([gright_ref[2 * g, rows, lanes], gright_ref[2 * g + 1, rows, lanes]], axis=0)

    def pack_right(seq, _):
        cy, cx, cz = seq // 8, (seq // 4) % 2, seq % 4
        for lo in range(2):
            for g in range(4):
                sib_r[cx * 2 + lo, cy, cz, g * 16 : g * 16 + 16, :] = right_tile(seq, lo, g, other_r).astype(BF)
        return _

    lax.fori_loop(0, SEQ, pack_left, 0)
    first_l = remote(sib_l, got_l, core_sems.at[0, 0], core_sems.at[1, 0], sibling)
    first_l.start()
    lax.fori_loop(0, SEQ, pack_right, 0)
    first_r = remote(sib_r, got_r, core_sems.at[0, 1], core_sems.at[1, 1], sibling)
    first_r.start()

    def sum_left(seq, _):
        cy, cx, cz = seq // 8, (seq // 4) % 2, seq % 4
        left_piece(seq, half_l)
        for lo in range(2):
            value = piece[lo * 32 : lo * 32 + 32, :] + got_l[cx * 2 + lo, cy, cz].astype(F32)
            own_l[cx * 2 + lo, cy, cz] = value.astype(BF)
        return _

    def sum_right(seq, _):
        cy, cx, cz = seq // 8, (seq // 4) % 2, seq % 4
        for lo in range(2):
            for g in range(4):
                rows = slice(g * 16, g * 16 + 16)
                value = right_tile(seq, lo, g, half_r) + got_r[cx * 2 + lo, cy, cz, rows, :].astype(F32)
                own_r[cx * 2 + lo, cy, cz, rows, :] = value.astype(BF)
        return _

    first_l.wait()
    lax.fori_loop(0, SEQ, sum_left, 0)
    first_r.wait()
    lax.fori_loop(0, SEQ, sum_right, 0)

    parts = [(own_l, (d0_l, d1_l, d2_l), full_l, core) + part for part in LEFT_PARTS] + [
        (own_r, (d0_r, d1_r, d2_r), full_r, core * 2) + part for part in RIGHT_PARTS
    ]
    stages = {}

    def add(number, stage):
        buf, heaps, full, first_lane, row, rows, order = parts[number]
        rest = order[stage + 1 :]
        span = pl.ds(row, rows)

        def one(i, _):
            at = {order[n]: xyz[order[n]] for n in range(stage + 1)}
            spots = []
            left_over = i
            for axis in reversed(sorted(rest)):
                at[axis] = left_over % 4
                spots.insert(0, left_over % 4)
                left_over = left_over // 4
            index = (at[0], at[1], at[2], span)
            value = buf[index].astype(F32)
            for step in range(3):
                value = value + heaps[stage][(step, *spots, span)].astype(F32)
            if stage == 2:
                for n in range(value.shape[1] // LANE):
                    full[first_lane + n, span, :] = value[:, n * LANE : (n + 1) * LANE]
            else:
                buf[index] = value.astype(BF)
            return _

        if rest:
            lax.fori_loop(0, 4 ** len(rest), one, 0)
        else:
            one(0, 0)

    for stage in range(4):
        for number, (buf, heaps, _, _, row, rows, order) in enumerate(parts):
            if stage > 0:
                for copy in stages[number]:
                    copy.wait()
                add(number, stage - 1)
            if stage == 3:
                continue
            span = pl.ds(row, rows)
            stages[number] = []
            for step in (1, 2, 3):
                to = moved(xyz, order[stage], step)
                index = tuple(slice(None) if axis in order[stage + 1 :] else to[axis] for axis in range(3))
                heap = heaps[stage].at[(step - 1,) + (slice(None),) * (2 - stage) + (span,)]
                stages[number].append(
                    remote(
                        buf.at[index + (span,)],
                        heap,
                        axis_sems.at[0, number, stage, step - 1],
                        axis_sems.at[1, number, stage, step - 1],
                        device_at(to, core),
                    )
                )
            for copy in stages[number]:
                copy.start()
    last = [
        remote(full_l.at[core], full_l.at[core], core_sems.at[0, 2], core_sems.at[1, 2], sibling),
        remote(full_r.at[pl.ds(core * 2, 2)], full_r.at[pl.ds(core * 2, 2)], core_sems.at[0, 3], core_sems.at[1, 3], sibling),
    ]
    for copy in last:
        copy.start()
    for copy in last:
        copy.wait()
    for lane in range(4):
        lanes = slice(lane * LANE, (lane + 1) * LANE)
        for r in range(4):
            right_out[r, :, lanes] = full_r[lane, pl.ds(core * 4 + r, 8, stride=8), :] / math.sqrt(A * C / H)
        if lane < 2:
            for r in range(2):
                left_out[r, :, lanes] = full_l[lane, pl.ds(core * 2 + r, 8, stride=4), :] / math.sqrt(B * C / H)


def reduce_tiles(gright, gleft):
    vmem = pl.BlockSpec(memory_space=pltpu.VMEM)
    return pl.pallas_call(
        reduce_kernel,
        out_shape=(jax.ShapeDtypeStruct((4, H, B), F32), jax.ShapeDtypeStruct((2, H, A), F32)),
        in_specs=[vmem, vmem],
        out_specs=(vmem, vmem),
        scratch_shapes=[
            pltpu.VMEM((4, 4, 4, 64, 256), BF),
            pltpu.VMEM((4, 4, 4, 32, 128), BF),
            pltpu.VMEM((4, 4, 4, 64, 256), BF),
            pltpu.VMEM((4, 4, 4, 32, 128), BF),
            pltpu.VMEM((4, 4, 4, 64, 256), BF),
            pltpu.VMEM((4, 4, 4, 32, 128), BF),
            pltpu.VMEM((3, 4, 4, 64, 256), BF),
            pltpu.VMEM((3, 4, 64, 256), BF),
            pltpu.VMEM((3, 64, 256), BF),
            pltpu.VMEM((3, 4, 4, 32, 128), BF),
            pltpu.VMEM((3, 4, 32, 128), BF),
            pltpu.VMEM((3, 32, 128), BF),
            pltpu.VMEM((4, 64, LANE), F32),
            pltpu.VMEM((2, 32, LANE), F32),
            pltpu.VMEM((64, LANE), F32),
            pltpu.SemaphoreType.DMA((2, 4)),
            pltpu.SemaphoreType.DMA((2, 4, 3, 3)),
        ],
        compiler_params=pltpu.CompilerParams(collective_id=2, has_side_effects=True, vmem_limit_bytes=48 << 20),
        name="reduce_tiles",
    )(gright, gleft)


def on_device(inputs, gate_values, kernel, grad_out, left_tiles, right_tiles):
    right, left = gather_tiles(right_tiles.reshape(32, B), left_tiles.reshape(16, A))
    output, grad_inputs, grad_gates, grad_kernel, gleft, gright = mix(
        inputs, gate_values, kernel, grad_out, right, left
    )
    grad_right, grad_left = reduce_tiles(gright, gleft)
    return (output, grad_inputs, grad_gates, grad_kernel, grad_left, grad_right)


def solution(mesh):
    specs = (P("seq", None, "chan"),) * 4 + (P(("seq", "chan"), None, None),) * 2
    return jax.shard_map(on_device, mesh=mesh, in_specs=specs, out_specs=specs, check_vma=False)
```

time: 1880 us -> 214 us (0.11)
  waiting for transfers between devices: 1530 us -> 0 us
  Pallas kernels: 0 us -> 194 us
  local copies, waits for them, and re-layouts: 205 us -> 17.9 us
  blocking collectives: 46.7 us -> 0 us
  matrix products: 44.8 us -> 0 us
  other arithmetic: 30.4 us -> 0 us
    reduce_scatter x2 -> x0, waiting for transfers between devices: 1240 us -> none  [the longest x1 645 us: on_device(): lax.psum_scatter(jnp.einsum('apdh,abdh->phb', block, gated_four, preferre...]
    all_gather x2 -> x0, waiting for transfers between devices: 261 us -> none  [the longest x1 191 us: on_device(): lax.all_gather(left_tiles, ('seq', 'chan'), axis=0, tiled=True)]
    pallas_call x0 -> x3, Pallas kernels: none -> 194 us  [the longest x1 110 us: mix(): pl.pallas_call(main_kernel, out_shape=(jax.ShapeDtypeStruct((16, A, 384),...]
    unnamed x26 -> x24, local copies, waits for them, and re-layouts: 94 us -> 17.9 us
    convert_element_type x7 -> x0, local copies, waits for them, and re-layouts: 67.4 us -> none  [the longest x3 36.9 us: on_device(): back_float = back_local.astype(jnp.float32)]
    all_to_all x1 -> x0, blocking collectives: 46.7 us -> none  [on_device(): lax.all_to_all(twisted, 'seq', split_axis=1, concat_axis=0, tiled=True)]
    dot_general x6 -> x0, matrix products: 44.8 us -> none  [the longest x1 14.6 us: on_device(): jnp.einsum('phb,abdh->apdh', lax.all_gather(right_tiles, ('seq', 'chan'),...]
    all_to_all x3 -> x0, local copies, waits for them, and re-layouts: 30.5 us -> none  [the longest x2 19.6 us: on_device(): lax.all_to_all(twisted, 'seq', split_axis=1, concat_axis=0, tiled=True)]
  transfers between devices with their start and end apart: 5 -> 0, of which waited for: 5 -> 0; matrix products, arithmetic and copies ran while one was open for 9% -> 0% of each run, Pallas kernels for 0% -> 0%
where the time goes in v1:
time: 214 us; the launch traced here: 212 us
  Pallas kernels  194 us (91%)
  local copies, waits for them, and re-layouts  17.9 us (8%)
    pallas_call x1, Pallas kernels, mix(): pl.pallas_call(main_kernel, out_shape=(jax.ShapeDtypeStruct((16, A, 384),...  110 us
    pallas_call x1, Pallas kernels, reduce_tiles(): pl.pallas_call(reduce_kernel, out_shape=(jax.ShapeDtypeStruct((4, H, B),...  46.8 us
    pallas_call x1, Pallas kernels, gather_tiles(): pl.pallas_call(gather_kernel, out_shape=(jax.ShapeDtypeStruct((H, B, B),...  37.5 us
    unnamed x24, local copies, waits for them, and re-layouts  17.9 us

profile of v1, /device:TPU:0, one launch (start us, length us, event | category | flops | bytes accessed | tf_op | source)
XLA Modules:
  0.0 212.5 jit_solution(4131300432400813277)
XLA Ops:
  0.6 0.0 copy-start.3
  0.6 0.7 copy-done.3
  1.4 0.0 copy-start.4
  1.4 0.7 copy-done.4
  2.1 37.5 %gather_tiles.1 = (bf16[8,512,512]{2,1,0:T(8,128)(2,1)S(1)}, bf16[8,256,256]{2,1,0:T(8,128)(2,1)S(1)}) custom-call(bf16[32,512]{1,0:T(8,128)(2,1)S(1)} %bitcast.2, bf16[16,256]{1,0:T(8,128)(2,1)S(1)} %bitcast.3), custom_call_target="tpu_custom_call" | custom-call | tf_op jit(solution)/shard_map/gather_tiles/pallas_call | solution.py:151
  39.6 0.0 copy-start
  39.6 2.0 copy-done
  41.6 0.0 copy-start.2
  41.6 1.0 copy-done.2
  42.5 109.5 %mix.1 = (bf16[16,256,384]{2,1,0:T(8,128)(2,1)}, bf16[8,512,384]{2,1,0:T(8,128)(2,1)}, bf16[8,512,384]{2,1,0:T(8,128)(2,1)}, bf16[8,512,384]{2,1,0:T(8,128)(2,1)...) custom-call(bf16[8,512,384]{2,1,0:T(8,128)(2,1)} %in_ref.1, bf16[8,512,384]{2,1,0:T(8,128)(2,1)} %gate_ref.1, ...), custom_call_target="tpu_custom_call" | custom-call | tf_op jit(solution)/shard_map/mix/pallas_call | solution.py:452
  152.0 0.0 copy-start.1
  152.0 1.6 copy-done.1
  153.6 46.8 %reduce_tiles.1 = (f32[4,8,512]{2,1,0:T(8,128)S(1)}, f32[2,8,256]{2,1,0:T(8,128)S(1)}) custom-call(f32[8,512,512]{2,1,0:T(8,128)} %get-tuple-element.22.gright_ref, f32[8,256,256]{2,1,0:T(8,128)S(1)} %copy-done.1), custom_call_target="tpu_custom_call" | custom-call | tf_op jit(solution)/shard_map/reduce_tiles/pallas_call | solution.py:626
  200.5 0.0 copy-done.8
  200.5 0.0 copy-start.7
  200.5 1.7 copy.18
  202.2 1.3 copy-done.7
  203.5 1.7 copy.19
  205.2 1.4 copy-done.6
  206.6 1.7 copy.20
  208.2 1.4 copy-done.5
  209.6 1.7 copy.21
  211.2 0.6 copy.22
  211.8 0.6 copy.23
  (3 shorter events, 0.0 us)
Async XLA Ops:
  0.6 0.8 copy-start.3
  1.4 0.7 copy-start.4
  39.6 2.0 copy-start
  41.6 1.0 copy-start.2
  152.0 1.6 copy-start.1
  153.6 46.9 %copy-start.8 = (bf16[16,256,384]{2,1,0:T(8,128)(2,1)S(1)}, bf16[16,256,384]{2,1,0:T(8,128)(2,1)}, u32[]{:S(2)}) copy-start(bf16[16,256,384]{2,1,0:T(8,128)(2,1)} %get-tuple-element.32) | copy-start | bytes 9437188
  200.5 3.0 %copy-start.7 = (bf16[8,512,384]{2,1,0:T(8,128)(2,1)S(1)}, bf16[8,512,384]{2,1,0:T(8,128)(2,1)}, u32[]{:S(2)}) copy-start(bf16[8,512,384]{2,1,0:T(8,128)(2,1)} %get-tuple-element.33) | copy-start | bytes 9437188
  203.5 3.0 %copy-start.6 = (bf16[8,512,384]{2,1,0:T(8,128)(2,1)S(1)}, bf16[8,512,384]{2,1,0:T(8,128)(2,1)}, u32[]{:S(2)}) copy-start(bf16[8,512,384]{2,1,0:T(8,128)(2,1)} %get-tuple-element.34) | copy-start | bytes 9437188
  206.5 3.0 %copy-start.5 = (bf16[8,512,384]{2,1,0:T(8,128)(2,1)S(1)}, bf16[8,512,384]{2,1,0:T(8,128)(2,1)}, u32[]{:S(2)}) copy-start(bf16[8,512,384]{2,1,0:T(8,128)(2,1)} %get-tuple-element.35) | copy-start | bytes 9437188

commit v2 on v0

v2 whole, which is shorter than its diff:
```python
import functools
import math

import jax
import jax.numpy as jnp
from jax import lax
from jax.experimental import pallas as pl
from jax.experimental.pallas import tpu as pltpu
from jax.sharding import PartitionSpec as P

MESH = pl.DeviceIdType.MESH
BF = jnp.bfloat16
F32 = jnp.float32
A = 256
B = 512
C = 1536
H = 8
LANE = 128
SEQ = 32
RIGHT_PARTS = ((0, 256, (0, 1, 2)), (256, 128, (1, 2, 0)), (384, 128, (2, 0, 1)))
LEFT_PARTS = ((0, 128, (1, 2, 0)), (128, 128, (2, 0, 1)))


def place():
    seq = lax.axis_index("seq")
    chan = lax.axis_index("chan")
    x = ((seq // 4) % 2) * 2 + chan // 2
    return (x, seq // 8, seq % 4), chan % 2


def device_at(xyz, core):
    x, y, z = xyz
    return (y * 8 + (x // 2) * 4 + z, (x % 2) * 2 + core)


def moved(xyz, axis, step):
    new = list(xyz)
    new[axis] = (xyz[axis] + step) % 4
    return tuple(new)


def chip_friends(xyz, core):
    return [device_at(xyz, 1 - core)] + [
        device_at(moved(xyz, axis, step), core) for axis in range(3) for step in (1, 2, 3)
    ]


def remote(src, dst, send, recv, device):
    return pltpu.make_async_remote_copy(
        src_ref=src, dst_ref=dst, send_sem=send, recv_sem=recv, device_id=device, device_id_type=MESH
    )


def aligned(value, multiple):
    return pl.multiple_of(value, multiple)


def masks_of(rows):
    lane = lax.broadcasted_iota(jnp.int32, (rows, LANE), 1)
    return [(lane & bit) != 0 for bit in (1, 2, 4)]


def turn(values, masks):
    for bit, mask in zip((1, 2, 4), masks):
        values = [jnp.where(mask, values[(i + bit) % 8], values[i]) for i in range(8)]
    return values


def to_groups(values, masks):
    values = turn([v if n == 0 else pltpu.roll(v, n, 1) for n, v in enumerate(values)], masks)
    return [values[(-h) % 8] for h in range(8)]


def from_groups(values, masks):
    values = turn(values, masks)
    return [values[0]] + [pltpu.roll(values[(-n) % 8], LANE - n, 1) for n in range(1, 8)]


def dot(a, b, ca, cb):
    return lax.dot_general(a, b, (((ca,), (cb,)), ((), ())), preferred_element_type=F32)


def seq_offset(k):
    return (k * 11) % SEQ


def seq_moved(seq, off):
    y, xh, z = seq // 8, (seq // 4) % 2, seq % 4
    dy, dx, dz = off // 8, (off // 4) % 2, off % 4
    return ((y + dy) % 4) * 8 + ((xh + dx) % 2) * 4 + (z + dz) % 4


class Exchange:
    def __init__(self, src, dst, send, recv, local):
        self.src, self.dst, self.send, self.recv, self.local = src, dst, send, recv, local

    def copy(self, j, k):
        me = lax.axis_index("seq")
        peer = seq_moved(me, seq_offset(k))
        lanes = pl.ds(j * LANE, LANE)
        return remote(
            self.src.at[:, pl.ds(aligned(peer * 16, 16), 16), lanes],
            self.dst.at[:, pl.ds(aligned(me * 16, 16), 16), lanes],
            self.send.at[j, k],
            self.recv.at[j, k],
            (peer, lax.axis_index("chan")),
        )

    def own(self, j):
        rows = pl.ds(aligned(lax.axis_index("seq") * 16, 16), 16)
        lanes = pl.ds(j * LANE, LANE)
        return pltpu.make_async_copy(self.src.at[:, rows, lanes], self.dst.at[:, rows, lanes], self.local.at[j])

    def start(self, j):
        def step(k, _):
            self.copy(j, k).start()
            return _

        lax.fori_loop(1, SEQ, step, 0)
        self.own(j).start()

    def arrived(self, j):
        def step(k, _):
            self.copy(j, k).wait_recv()
            return _

        self.own(j).wait()
        lax.fori_loop(1, SEQ, step, 0)

    def sent(self, j):
        def step(k, _):
            self.copy(j, k).wait_send()
            return _

        lax.fori_loop(1, SEQ, step, 0)


class Gather:
    def __init__(self, buf, rows, lane, lanes, order, send, recv):
        self.buf, self.rows, self.lanes, self.order = buf, rows, pl.ds(lane, lanes), order
        self.send, self.recv = send, recv

    def copies(self, stage):
        xyz, core = place()
        index = tuple(slice(None) if axis in self.order[:stage] else xyz[axis] for axis in range(3))
        ref = self.buf.at[index + (pl.ds(aligned(core * self.rows, self.rows), self.rows), self.lanes)]
        return [
            remote(
                ref,
                ref,
                self.send.at[stage, step - 1],
                self.recv.at[stage, step - 1],
                device_at(moved(xyz, self.order[stage], step), core),
            )
            for step in (1, 2, 3)
        ]

    def start(self, stage):
        for copy in self.copies(stage):
            copy.start()

    def wait(self, stage):
        for copy in self.copies(stage):
            copy.wait()


class Reduce:
    def __init__(self, buf, heaps, out, scale, lane, lanes, order, send, recv):
        self.buf, self.heaps, self.out, self.scale = buf, heaps, out, scale
        self.lanes, self.order, self.send, self.recv = pl.ds(lane, lanes), order, send, recv

    def copies(self, stage):
        xyz, core = place()
        axis = self.order[stage]
        found = []
        for step in (1, 2, 3):
            to = moved(xyz, axis, step)
            index = tuple(slice(None) if n in self.order[stage + 1 :] else to[n] for n in range(3))
            found.append(
                remote(
                    self.buf.at[index + (slice(None), self.lanes)],
                    self.heaps[stage].at[(step - 1,) + (slice(None),) * (3 - stage) + (self.lanes,)],
                    self.send.at[stage, step - 1],
                    self.recv.at[stage, step - 1],
                    device_at(to, core),
                )
            )
        return found

    def start(self, stage):
        for copy in self.copies(stage):
            copy.start()

    def finish(self, stage):
        for copy in self.copies(stage):
            copy.wait()
        xyz, _ = place()
        rest = sorted(self.order[stage + 1 :])

        def one(i, carry):
            at = list(xyz)
            spots = [i // 4, i % 4][2 - len(rest) :]
            for axis, spot in zip(rest, spots):
                at[axis] = spot
            index = (*at, slice(None), self.lanes)
            value = self.buf[index].astype(F32)
            for step in range(3):
                value = value + self.heaps[stage][(step, *spots, slice(None), self.lanes)].astype(F32)
            if stage == 2:
                self.out[:, self.lanes] = value / self.scale
            else:
                self.buf[index] = value.astype(BF)
            return carry

        if rest:
            lax.fori_loop(0, 4 ** len(rest), one, 0)
        else:
            one(0, 0)


def blocks(body, j):
    def step(i, _):
        body(i, aligned(i * 16, 16), slice(j * LANE, (j + 1) * LANE))
        return _

    lax.fori_loop(0, 32, step, 0)


def chip_of(seq):
    return ((seq // 4) % 2) * 2, seq // 8, seq % 4


def layer_kernel(
    in_ref, gate_ref, ker_ref, cot_ref, right_ref, left_ref,
    out_ref, gin_ref, ggate_ref, gker_ref, gleft_ref, gright_ref,
    xin, xgate, xker, cot, gated, bsend, brecv, tsend, trecv, right, left, work, gsum, piece, raw_r, raw_l,
    own_r, sib_r, got_r, d0_r, d1_r, d2_r, own_l, sib_l, got_l, d0_l, d1_l, d2_l,
    load, own, sems, stores, core_sems, gather_sems, reduce_sems,
):
    me = lax.axis_index("seq")
    chan = lax.axis_index("chan")
    xyz, core = place()
    sibling = device_at(xyz, 1 - core)
    barrier = pltpu.get_barrier_semaphore()
    tgrp = bsend

    loads = {
        "cot0": pltpu.make_async_copy(cot_ref.at[pl.ds(0, 8)], cot.at[:, pl.ds(0, 256), :], load.at[0]),
        "cot1": pltpu.make_async_copy(cot_ref.at[pl.ds(8, 8)], cot.at[:, pl.ds(256, 256), :], load.at[1]),
        "in": pltpu.make_async_copy(in_ref, xin, load.at[2]),
        "gate": pltpu.make_async_copy(gate_ref, xgate, load.at[3]),
        "ker": pltpu.make_async_copy(ker_ref, xker, load.at[4]),
        "left": pltpu.make_async_copy(
            left_ref, raw_l.at[(*xyz, pl.ds(aligned(core * 16, 16), 16))], load.at[5]
        ),
        "right": pltpu.make_async_copy(
            right_ref, raw_r.at[(*xyz, pl.ds(aligned(core * 32, 32), 32))], load.at[6]
        ),
    }

    def hello(k, _):
        pl.semaphore_signal(barrier, inc=1, device_id=(seq_moved(me, seq_offset(k)), chan), device_id_type=MESH)
        return _

    lax.fori_loop(1, SEQ, hello, 0)
    friends = chip_friends(xyz, core)
    for device in friends:
        pl.semaphore_signal(barrier, inc=1, device_id=device, device_id_type=MESH)
    for name in ("left", "right", "cot0", "cot1", "in", "gate", "ker"):
        loads[name].start()
    pl.semaphore_wait(barrier, SEQ - 1 + len(friends))
    loads["left"].wait()
    loads["right"].wait()
    masks = masks_of(16)

    gather_l = [
        Gather(raw_l, 16, *part, gather_sems.at[0, n], gather_sems.at[1, n]) for n, part in enumerate(LEFT_PARTS)
    ]
    gather_r = [
        Gather(raw_r, 32, *part, gather_sems.at[0, 2 + n], gather_sems.at[1, 2 + n])
        for n, part in enumerate(RIGHT_PARTS)
    ]
    mine_l = raw_l.at[:, :, :, pl.ds(aligned(core * 16, 16), 16), :]
    mine_r = raw_r.at[:, :, :, pl.ds(aligned(core * 32, 32), 32), :]
    swap_l = remote(mine_l, mine_l, core_sems.at[0, 0], core_sems.at[1, 0], sibling)
    swap_r = remote(mine_r, mine_r, core_sems.at[0, 1], core_sems.at[1, 1], sibling)
    back = Exchange(bsend, brecv, sems.at[0], sems.at[1], own.at[0])
    twisted = Exchange(tsend, trecv, sems.at[2], sems.at[3], own.at[1])

    def cot_groups(i, row, lanes):
        values = [cot[n, pl.ds(row, 16), lanes].astype(F32) for n in range(8)]
        for h, value in enumerate(to_groups(values, masks)):
            cot[h, pl.ds(row, 16), lanes] = value.astype(BF)

    for part in gather_l + gather_r:
        part.start(0)
    loads["cot0"].wait()
    loads["cot1"].wait()
    blocks(cot_groups, 0)
    for stage in range(2):
        for part in gather_l:
            part.wait(stage)
            part.start(stage + 1)
        if stage == 0:
            for part in gather_r:
                part.wait(0)
                part.start(1)
        blocks(cot_groups, stage + 1)
    for part in gather_l:
        part.wait(2)
    swap_l.start()
    for part in gather_r:
        part.wait(1)
        part.start(2)
    swap_l.wait()

    def left_rows(pair, _):
        cx, cy, cz = chip_of(pair * 2)
        for lane in range(2):
            lanes = slice(lane * LANE, (lane + 1) * LANE)
            for n in range(4):
                piece[lane, n * 32 : n * 32 + 32, :] = raw_l[cx + n % 2, cy, cz + n // 2, :, lanes].astype(F32)
            for h in range(H):
                left[h, pl.ds(aligned(pair * 16, 16), 16), lanes] = piece[lane, pl.ds(h, 16, stride=8), :].astype(BF)
        return _

    lax.fori_loop(0, 16, left_rows, 0)

    def both(ref, h, lanes):
        return jnp.concatenate([ref[h, :256, lanes], ref[h, 256:, lanes]], axis=1)

    def back_rows(j):
        lanes = slice(j * LANE, (j + 1) * LANE)

        def product(h, _):
            value = dot(left[h], both(cot, h, lanes), 0, 0)
            work[j, pl.ds(aligned(h * 512, 512), 256), :] = value[:, :LANE]
            work[j, pl.ds(aligned(h * 512 + 256, 256), 256), :] = value[:, LANE:]
            return _

        lax.fori_loop(0, H, product, 0)

        def rows(i, _):
            for half in range(2):
                values = [work[j, pl.ds(aligned(h * 512 + half * 256 + i * 16, 16), 16), :] for h in range(8)]
                for n, value in enumerate(from_groups(values, masks)):
                    piece[j, pl.ds(half * 8 + n, 16, stride=16), :] = value
            for k in range(16):
                to = aligned((2 * i + k // 8) * 16, 16)
                bsend[k % 8, pl.ds(to, 16), lanes] = piece[j, k * 16 : k * 16 + 16, :].astype(BF)
            return _

        lax.fori_loop(0, 16, rows, 0)

    for j in range(3):
        back_rows(j)
        back.start(j)

    loads["in"].wait()
    loads["gate"].wait()

    def gate_groups(i, row, lanes):
        rows = pl.ds(row, 16)
        values = [xin[n, rows, lanes].astype(F32) * xgate[n, rows, lanes].astype(F32) for n in range(8)]
        for h, value in enumerate(to_groups(values, masks)):
            gated[h, rows, lanes] = value.astype(BF)

    for j in range(3):
        blocks(gate_groups, j)
    for part in gather_r:
        part.wait(2)
    swap_r.start()
    loads["ker"].wait()
    swap_r.wait()

    def right_rows(seq, _):
        cx, cy, cz = chip_of(seq)
        for lane in range(4):
            lanes = slice(lane * LANE, (lane + 1) * LANE)
            for lo in range(2):
                piece[lane, lo * 64 : lo * 64 + 64, :] = raw_r[cx + lo, cy, cz, :, lanes].astype(F32)
            for h in range(H):
                right[h, pl.ds(aligned(seq * 16, 16), 16), lanes] = piece[lane, pl.ds(h, 16, stride=8), :].astype(BF)
        return _

    lax.fori_loop(0, 32, right_rows, 0)

    def spread(h, value):
        for j in range(3):
            work[j, pl.ds(aligned(h * 512, 512), 512), :] = value[:, j * LANE : (j + 1) * LANE]

    def inner_dot(h, _):
        spread(h, dot(right[h], gated[h], 1, 0))
        return _

    lax.fori_loop(0, H, inner_dot, 0)

    def group_rows(j, row):
        return [work[j, pl.ds(aligned(h * 512 + row, 16), 16), :] for h in range(8)]

    def twist(j):
        def body(i, row, lanes):
            rows = pl.ds(row, 16)
            for n, value in enumerate(from_groups(group_rows(j, row), masks)):
                work[j, pl.ds(aligned(n * 512 + row, 16), 16), :] = value
                tsend[n, rows, lanes] = (xker[n, rows, lanes].astype(F32) * value).astype(BF)

        blocks(body, j)

    def push(j):
        def body(i, row, lanes):
            rows = pl.ds(row, 16)
            values = []
            spectral = group_rows(j, row)
            for n in range(8):
                value = brecv[n, rows, lanes].astype(F32)
                weight = xker[n, rows, lanes].astype(F32)
                xker[n, rows, lanes] = (value * spectral[n]).astype(BF)
                values.append(weight * value)
            for h, value in enumerate(to_groups(values, masks)):
                brecv[h, rows, lanes] = value.astype(BF)

        blocks(body, j)

    for j in range(3):
        twist(j)
    for j in range(3):
        back.arrived(j)
        twisted.start(j)
        push(j)
    save = [pltpu.make_async_copy(xker, gker_ref, stores.at[0])]
    save[0].start()

    def pack_right(block):
        def product(h, _):
            value = dot(brecv[h, block * 128 : block * 128 + 128, :], gated[h], 1, 1)
            for lane in range(4):
                row = aligned(h * 512 + lane * 128, 128)
                work[0, pl.ds(row, 128), :] = value[:, lane * LANE : (lane + 1) * LANE]
            return _

        lax.fori_loop(0, H, product, 0)

        def rows(n, _):
            cx, cy, cz = chip_of(block * 8 + n)
            for lane in range(4):
                lanes = slice(lane * LANE, (lane + 1) * LANE)
                for lo in range(2):
                    for buf, which in ((sib_r, 1 - core), (own_r, core)):
                        row = lane * 128 + n * 16 + lo * 8 + which * 4
                        for half in range(2):
                            tile = jnp.concatenate(
                                [work[0, pl.ds(row + half * 2 + r, 8, stride=512), :] for r in range(2)], axis=0
                            )
                            buf[cx + lo, cy, cz, half * 16 : half * 16 + 16, lanes] = tile.astype(BF)
            return _

        lax.fori_loop(0, 8, rows, 0)

    for block in range(4):
        pack_right(block)
    pair_r = remote(sib_r, got_r, core_sems.at[0, 2], core_sems.at[1, 2], sibling)
    pair_r.start()
    reduce_r = [
        Reduce(own_r, (d0_r, d1_r, d2_r), gright_ref, math.sqrt(A * C / H), *part, reduce_sems.at[0, 2 + n], reduce_sems.at[1, 2 + n])
        for n, part in enumerate(RIGHT_PARTS)
    ]
    reduce_l = [
        Reduce(own_l, (d0_l, d1_l, d2_l), gleft_ref, math.sqrt(B * C / H), *part, reduce_sems.at[0, n], reduce_sems.at[1, n])
        for n, part in enumerate(LEFT_PARTS)
    ]

    def gated_dot(h, _):
        spread(h, dot(right[h], brecv[h], 0, 0))
        return _

    lax.fori_loop(0, H, gated_dot, 0)
    pair_r.wait()

    def add_pair(i, _):
        index = (i // 16, (i // 4) % 4, i % 4)
        own_r[index] = (own_r[index].astype(F32) + got_r[index].astype(F32)).astype(BF)
        return _

    lax.fori_loop(0, 64, add_pair, 0)
    for part in reduce_r:
        part.start(0)

    def gate_grads(j):
        def body(i, row, lanes):
            rows = pl.ds(row, 16)
            for n, value in enumerate(from_groups(group_rows(j, row), masks)):
                first = xin[n, rows, lanes].astype(F32)
                second = xgate[n, rows, lanes].astype(F32)
                xin[n, rows, lanes] = (value * second).astype(BF)
                xgate[n, rows, lanes] = (value * first).astype(BF)

        blocks(body, j)

    for j in range(3):
        gate_grads(j)
    save.append(pltpu.make_async_copy(xin, gin_ref, stores.at[1]))
    save.append(pltpu.make_async_copy(xgate, ggate_ref, stores.at[2]))
    save[1].start()
    save[2].start()
    for j in range(3):
        back.sent(j)

    def twist_groups(j):
        lanes = slice(j * LANE, (j + 1) * LANE)

        def rows(i, _):
            for k in range(16):
                at = aligned((2 * i + k // 8) * 16, 16)
                piece[j, k * 16 : k * 16 + 16, :] = trecv[k % 8, pl.ds(at, 16), lanes].astype(F32)
            for half in range(2):
                values = [piece[j, pl.ds(half * 8 + n, 16, stride=16), :] for n in range(8)]
                for h, value in enumerate(to_groups(values, masks)):
                    tgrp[h, pl.ds(aligned(half * 256 + i * 16, 16), 16), lanes] = value.astype(BF)
            return _

        lax.fori_loop(0, 16, rows, 0)

    def left_terms(j):
        lanes = slice(j * LANE, (j + 1) * LANE)

        def product(h, _):
            value = dot(both(cot, h, lanes), both(tgrp, h, lanes), 1, 1)
            rows = pl.ds(aligned(h * 256, 256), 256)
            for lane in range(2):
                term = value[:, lane * LANE : (lane + 1) * LANE]
                gsum[lane, rows, :] = term if j == 0 else gsum[lane, rows, :] + term
            return _

        lax.fori_loop(0, H, product, 0)

    def outer(j):
        lanes = slice(j * LANE, (j + 1) * LANE)

        def product(h, _):
            value = dot(left[h], both(tgrp, h, lanes), 1, 0)
            work[j, pl.ds(aligned(h * 512, 512), 256), :] = value[:, :LANE]
            work[j, pl.ds(aligned(h * 512 + 256, 256), 256), :] = value[:, LANE:]
            return _

        lax.fori_loop(0, H, product, 0)

        def body(i, row, lanes):
            for n, value in enumerate(from_groups(group_rows(j, row), masks)):
                trecv[n, pl.ds(row, 16), lanes] = value.astype(BF)

        blocks(body, j)

    for j in range(3):
        twisted.arrived(j)
        twist_groups(j)
        left_terms(j)
        if j < 2:
            for part in reduce_r:
                part.finish(j)
                part.start(j + 1)
            outer(j)

    def left_tile(seq, lo, which, lane):
        row = seq * 8 + lo * 4 + which * 2
        return jnp.concatenate([gsum[lane, pl.ds(row + r, 8, stride=256), :] for r in range(2)], axis=0)

    def pack_left(seq, _):
        cx, cy, cz = chip_of(seq)
        for lo in range(2):
            for lane in range(2):
                lanes = slice(lane * LANE, (lane + 1) * LANE)
                sib_l[cx + lo, cy, cz, :, lanes] = left_tile(seq, lo, 1 - core, lane).astype(BF)
        return _

    def add_left(seq, _):
        cx, cy, cz = chip_of(seq)
        for lo in range(2):
            for lane in range(2):
                lanes = slice(lane * LANE, (lane + 1) * LANE)
                value = left_tile(seq, lo, core, lane) + got_l[cx + lo, cy, cz, :, lanes].astype(F32)
                own_l[cx + lo, cy, cz, :, lanes] = value.astype(BF)
        return _

    lax.fori_loop(0, SEQ, pack_left, 0)
    pair_l = remote(sib_l, got_l, core_sems.at[0, 3], core_sems.at[1, 3], sibling)
    pair_l.start()
    for part in reduce_r:
        part.finish(2)
    pair_l.wait()
    lax.fori_loop(0, SEQ, add_left, 0)
    for part in reduce_l:
        part.start(0)
    outer(2)
    save.append(pltpu.make_async_copy(trecv.at[:, pl.ds(0, 256), :], out_ref.at[pl.ds(0, 8)], stores.at[3]))
    save.append(pltpu.make_async_copy(trecv.at[:, pl.ds(256, 256), :], out_ref.at[pl.ds(8, 8)], stores.at[4]))
    save[3].start()
    save[4].start()
    for stage in range(3):
        for part in reduce_l:
            part.finish(stage)
            if stage < 2:
                part.start(stage + 1)
    for j in range(3):
        twisted.sent(j)
    for copy in save:
        copy.wait()


def layer(inputs, gate_values, kernel, grad_out, right, left):
    hbm = pl.BlockSpec(memory_space=pl.ANY)
    vmem = pl.BlockSpec(memory_space=pltpu.VMEM)
    rows = pltpu.VMEM((8, B, 384), BF)

    def heap(rows, lanes):
        block = (rows, lanes)
        return [pltpu.VMEM((4, 4, 4) + block, BF)] * 3 + [
            pltpu.VMEM((3, 4, 4) + block, BF),
            pltpu.VMEM((3, 4) + block, BF),
            pltpu.VMEM((3,) + block, BF),
        ]

    return pl.pallas_call(
        layer_kernel,
        out_shape=(
            jax.ShapeDtypeStruct((16, A, 384), BF),
            jax.ShapeDtypeStruct((8, B, 384), BF),
            jax.ShapeDtypeStruct((8, B, 384), BF),
            jax.ShapeDtypeStruct((8, B, 384), BF),
            jax.ShapeDtypeStruct((16, A), F32),
            jax.ShapeDtypeStruct((32, B), F32),
        ),
        in_specs=[hbm] * 6,
        out_specs=(hbm,) * 4 + (vmem,) * 2,
        scratch_shapes=[rows] * 9
        + [
            pltpu.VMEM((H, B, B), BF),
            pltpu.VMEM((H, A, A), BF),
            pltpu.VMEM((3, H * B, LANE), F32),
            pltpu.VMEM((2, H * A, LANE), F32),
            pltpu.VMEM((4, 256, LANE), F32),
            pltpu.VMEM((4, 4, 4, 64, B), BF),
            pltpu.VMEM((4, 4, 4, 32, A), BF),
        ]
        + heap(32, B)
        + heap(16, A)
        + [
            pltpu.SemaphoreType.DMA((7,)),
            pltpu.SemaphoreType.DMA((2, 3)),
            pltpu.SemaphoreType.DMA((4, 3, SEQ)),
            pltpu.SemaphoreType.DMA((5,)),
            pltpu.SemaphoreType.DMA((2, 4)),
            pltpu.SemaphoreType.DMA((2, 5, 3, 3)),
            pltpu.SemaphoreType.DMA((2, 5, 3, 3)),
        ],
        compiler_params=pltpu.CompilerParams(collective_id=0, has_side_effects=True, vmem_limit_bytes=62 << 20),
        name="layer",
    )(inputs, gate_values, kernel, grad_out, right, left)


def on_device(inputs, gate_values, kernel, grad_out, left_tiles, right_tiles):
    output, grad_inputs, grad_gates, grad_kernel, grad_left, grad_right = layer(
        inputs, gate_values, kernel, grad_out, right_tiles.reshape(32, B), left_tiles.reshape(16, A)
    )
    return (
        output,
        grad_inputs,
        grad_gates,
        grad_kernel,
        grad_left.reshape(2, H, A),
        grad_right.reshape(4, H, B),
    )


def solution(mesh):
    specs = (P("seq", None, "chan"),) * 4 + (P(("seq", "chan"), None, None),) * 2
    return jax.shard_map(on_device, mesh=mesh, in_specs=specs, out_specs=specs, check_vma=False)
```

time: 1880 us -> 188 us (0.10)
  waiting for transfers between devices: 1530 us -> 0 us
  local copies, waits for them, and re-layouts: 205 us -> 13.1 us
  Pallas kernels: 0 us -> 174 us
  blocking collectives: 46.7 us -> 0 us
  matrix products: 44.8 us -> 0 us
  other arithmetic: 30.4 us -> 0 us
    reduce_scatter x2 -> x0, waiting for transfers between devices: 1240 us -> none  [the longest x1 645 us: on_device(): lax.psum_scatter(jnp.einsum('apdh,abdh->phb', block, gated_four, preferre...]
    all_gather x2 -> x0, waiting for transfers between devices: 261 us -> none  [the longest x1 191 us: on_device(): lax.all_gather(left_tiles, ('seq', 'chan'), axis=0, tiled=True)]
    pallas_call x0 -> x1, Pallas kernels: none -> 174 us  [layer(): pl.pallas_call(layer_kernel, out_shape=(jax.ShapeDtypeStruct((16, A, 384)...]
    unnamed x26 -> x16, local copies, waits for them, and re-layouts: 94 us -> 13.1 us
    convert_element_type x7 -> x0, local copies, waits for them, and re-layouts: 67.4 us -> none  [the longest x3 36.9 us: on_device(): back_float = back_local.astype(jnp.float32)]
    all_to_all x1 -> x0, blocking collectives: 46.7 us -> none  [on_device(): lax.all_to_all(twisted, 'seq', split_axis=1, concat_axis=0, tiled=True)]
    dot_general x6 -> x0, matrix products: 44.8 us -> none  [the longest x1 14.6 us: on_device(): jnp.einsum('phb,abdh->apdh', lax.all_gather(right_tiles, ('seq', 'chan'),...]
    all_to_all x3 -> x0, local copies, waits for them, and re-layouts: 30.5 us -> none  [the longest x2 19.6 us: on_device(): lax.all_to_all(twisted, 'seq', split_axis=1, concat_axis=0, tiled=True)]
  transfers between devices with their start and end apart: 5 -> 0, of which waited for: 5 -> 0; matrix products, arithmetic and copies ran while one was open for 9% -> 0% of each run, Pallas kernels for 0% -> 0%
where the time goes in v2:
time: 188 us
  Pallas kernels  174 us (93%)
  local copies, waits for them, and re-layouts  13.1 us (7%)
    pallas_call x1, Pallas kernels, layer(): pl.pallas_call(layer_kernel, out_shape=(jax.ShapeDtypeStruct((16, A, 384)...  174 us
    unnamed x16, local copies, waits for them, and re-layouts  13.1 us

profile of v2, /device:TPU:0, one launch (start us, length us, event | category | flops | bytes accessed | tf_op | source)
XLA Modules:
  0.0 188.0 jit_solution(14384912430057535630)
XLA Ops:
  0.6 174.3 %layer.1 = (bf16[16,256,384]{2,1,0:T(8,128)(2,1)}, bf16[8,512,384]{2,1,0:T(8,128)(2,1)}, bf16[8,512,384]{2,1,0:T(8,128)(2,1)}, bf16[8,512,384]{2,1,0:T(8,128)(2,...) custom-call(bf16[8,512,384]{2,1,0:T(8,128)(2,1)} %in_ref.1, bf16[8,512,384]{2,1,0:T(8,128)(2,1)} %gate_ref.1, ...), custom_call_target="tpu_custom_call" | custom-call | tf_op jit(solution)/shard_map/layer/pallas_call | solution.py:623
  174.9 0.0 copy-start.2
  175.0 4.1 %copy.18 = bf16[16,256,384]{2,1,0:T(8,128)(2,1)} copy(bf16[16,256,384]{2,1,0:T(8,128)(2,1)} %get-tuple-element.24) | data formatting | bytes 6291456
  179.1 0.0 copy-done.2
  179.1 0.0 copy-start.1
  179.1 1.7 copy.19
  180.7 1.4 copy-done.1
  182.1 0.0 copy-start
  182.1 1.7 copy.20
  183.8 1.4 copy-done
  185.1 0.0 copy-start.4
  185.1 0.0 copy-start.3
  185.1 1.7 copy.21
  186.8 0.0 copy-done.4
  186.8 0.6 copy.22
  187.4 0.0 copy-done.3
  187.4 0.6 copy.23
Async XLA Ops:
  174.9 4.1 %copy-start.2 = (bf16[8,512,384]{2,1,0:T(8,128)(2,1)S(1)}, bf16[8,512,384]{2,1,0:T(8,128)(2,1)}, u32[]{:S(2)}) copy-start(bf16[8,512,384]{2,1,0:T(8,128)(2,1)} %get-tuple-element.25) | copy-start | bytes 9437188
  179.1 3.0 %copy-start.1 = (bf16[8,512,384]{2,1,0:T(8,128)(2,1)S(1)}, bf16[8,512,384]{2,1,0:T(8,128)(2,1)}, u32[]{:S(2)}) copy-start(bf16[8,512,384]{2,1,0:T(8,128)(2,1)} %get-tuple-element.26) | copy-start | bytes 9437188
  182.1 3.0 %copy-start = (bf16[8,512,384]{2,1,0:T(8,128)(2,1)S(1)}, bf16[8,512,384]{2,1,0:T(8,128)(2,1)}, u32[]{:S(2)}) copy-start(bf16[8,512,384]{2,1,0:T(8,128)(2,1)} %get-tuple-element.27) | copy-start | bytes 9437188
  185.1 1.7 copy-start.4
  185.1 2.3 %copy-start.3 = (f32[32,512]{1,0:T(8,128)S(1)}, f32[32,512]{1,0:T(8,128)}, u32[]{:S(2)}) copy-start(f32[32,512]{1,0:T(8,128)} %get-tuple-element.17) | copy-start | bytes 196612

commit v3 on v2

--- a/solution.py
+++ b/solution.py
@@ -18,7 +18,6 @@
 LANE = 128
 SEQ = 32
 RIGHT_PARTS = ((0, 256, (0, 1, 2)), (256, 128, (1, 2, 0)), (384, 128, (2, 0, 1)))
-LEFT_PARTS = ((0, 128, (1, 2, 0)), (128, 128, (2, 0, 1)))
 
 
 def place():
@@ -81,7 +80,7 @@
 
 
 def seq_offset(k):
-    return (k * 11) % SEQ
+    return (k * 7) % SEQ
 
 
 def seq_moved(seq, off):
@@ -218,6 +217,99 @@
             one(0, 0)
 
 
+def plane_device(step):
+    (x, y, z), core = place()
+    return device_at((x, (y + step // 4) % 4, (z + step % 4) % 4), core)
+
+
+class PlaneGather:
+    def __init__(self, buf, lane, plane_first, axis_sems, plane_sems):
+        self.buf, self.lanes, self.plane_first = buf, pl.ds(lane, LANE), plane_first
+        self.axis_sems, self.plane_sems = axis_sems, plane_sems
+
+    def ref(self, stage):
+        (x, y, z), core = place()
+        spot = (x, y, z) if stage == 0 else (x, slice(None), slice(None)) if self.plane_first else (slice(None), y, z)
+        return self.buf.at[spot + (pl.ds(aligned(core * 16, 16), 16), self.lanes)]
+
+    def each(self, stage, act):
+        ref = self.ref(stage)
+        if self.plane_first == (stage == 0):
+
+            def one(step, carry):
+                act(remote(ref, ref, self.plane_sems.at[0, step], self.plane_sems.at[1, step], plane_device(step)))
+                return carry
+
+            lax.fori_loop(1, 16, one, 0)
+        else:
+            xyz, core = place()
+            for step in (1, 2, 3):
+                device = device_at(moved(xyz, 0, step), core)
+                act(remote(ref, ref, self.axis_sems.at[0, step], self.axis_sems.at[1, step], device))
+
+    def start(self, stage):
+        self.each(stage, lambda copy: copy.start())
+
+    def wait(self, stage):
+        self.each(stage, lambda copy: copy.wait())
+
+
+class PlaneReduce:
+    def __init__(self, buf, heaps, out, scale, lane, axis_first, axis_sems, plane_sems):
+        self.buf, self.heaps, self.out, self.scale = buf, heaps, out, scale
+        self.lanes, self.axis_first = pl.ds(lane, LANE), axis_first
+        self.axis_sems, self.plane_sems = axis_sems, plane_sems
+
+    def each(self, stage, act):
+        (x, y, z), core = place()
+        heap = self.heaps[stage]
+        if self.axis_first == (stage == 0):
+            spots = (slice(None), slice(None)) if stage == 0 else (y, z)
+            for step in (1, 2, 3):
+                to = (x + step) % 4
+                src = self.buf.at[(to,) + spots + (slice(None), self.lanes)]
+                sems = self.axis_sems.at[0, step], self.axis_sems.at[1, step]
+                act(remote(src, heap.at[step - 1], *sems, device_at((to, y, z), core)))
+        else:
+            spot = slice(None) if stage == 0 else x
+
+            def one(step, carry):
+                src = self.buf.at[spot, (y + step // 4) % 4, (z + step % 4) % 4, :, self.lanes]
+                sems = self.plane_sems.at[0, step], self.plane_sems.at[1, step]
+                act(remote(src, heap.at[step - 1], *sems, plane_device(step)))
+                return carry
+
+            lax.fori_loop(1, 16, one, 0)
+
+    def start(self, stage):
+        self.each(stage, lambda copy: copy.start())
+
+    def finish(self, stage):
+        self.each(stage, lambda copy: copy.wait())
+        (x, y, z), _ = place()
+        heap = self.heaps[stage]
+        count = 3 if self.axis_first == (stage == 0) else 15
+
+        def total(index, spots):
+            value = self.buf[(*index, slice(None), self.lanes)].astype(F32)
+            for step in range(count):
+                value = value + heap[(step, *spots)].astype(F32)
+            return value
+
+        if stage == 1:
+            self.out[:, self.lanes] = total((x, y, z), ()) / self.scale
+        elif self.axis_first:
+
+            def one(i, carry):
+                self.buf[x, i // 4, i % 4, :, self.lanes] = total((x, i // 4, i % 4), (i // 4, i % 4)).astype(BF)
+                return carry
+
+            lax.fori_loop(0, 16, one, 0)
+        else:
+            for n in range(4):
+                self.buf[n, y, z, :, self.lanes] = total((n, y, z), (n,)).astype(BF)
+
+
 def blocks(body, j):
     def step(i, _):
         body(i, aligned(i * 16, 16), slice(j * LANE, (j + 1) * LANE))
@@ -233,9 +325,9 @@
 def layer_kernel(
     in_ref, gate_ref, ker_ref, cot_ref, right_ref, left_ref,
     out_ref, gin_ref, ggate_ref, gker_ref, gleft_ref, gright_ref,
-    xin, xgate, xker, cot, gated, bsend, brecv, tsend, trecv, right, left, work, gsum, piece, raw_r, raw_l,
-    own_r, sib_r, got_r, d0_r, d1_r, d2_r, own_l, sib_l, got_l, d0_l, d1_l, d2_l,
-    load, own, sems, stores, core_sems, gather_sems, reduce_sems,
+    out, xin, xgate, xker, cot, gated, bsend, brecv, tsend, trecv, right, left, work, gsum, piece, raw_r, raw_l,
+    own_r, sib_r, got_r, d0_r, d1_r, d2_r, own_l, sib_l, got_l, a0_l, a1_l, b0_l, b1_l,
+    load, own, sems, stores, core_sems, gather_sems, reduce_sems, axis_sems, plane_sems,
 ):
     me = lax.axis_index("seq")
     chan = lax.axis_index("chan")
@@ -266,7 +358,7 @@
     friends = chip_friends(xyz, core)
     for device in friends:
         pl.semaphore_signal(barrier, inc=1, device_id=device, device_id_type=MESH)
-    for name in ("left", "right", "cot0", "cot1", "in", "gate", "ker"):
+    for name in ("left", "right", "cot0", "cot1"):
         loads[name].start()
     pl.semaphore_wait(barrier, SEQ - 1 + len(friends))
     loads["left"].wait()
@@ -274,10 +366,11 @@
     masks = masks_of(16)
 
     gather_l = [
-        Gather(raw_l, 16, *part, gather_sems.at[0, n], gather_sems.at[1, n]) for n, part in enumerate(LEFT_PARTS)
+        PlaneGather(raw_l, 0, True, axis_sems.at[0], plane_sems.at[0]),
+        PlaneGather(raw_l, LANE, False, axis_sems.at[1], plane_sems.at[1]),
     ]
     gather_r = [
-        Gather(raw_r, 32, *part, gather_sems.at[0, 2 + n], gather_sems.at[1, 2 + n])
+        Gather(raw_r, 32, *part, gather_sems.at[0, n], gather_sems.at[1, n])
         for n, part in enumerate(RIGHT_PARTS)
     ]
     mine_l = raw_l.at[:, :, :, pl.ds(aligned(core * 16, 16), 16), :]
@@ -297,17 +390,18 @@
     loads["cot0"].wait()
     loads["cot1"].wait()
     blocks(cot_groups, 0)
-    for stage in range(2):
-        for part in gather_l:
-            part.wait(stage)
-            part.start(stage + 1)
-        if stage == 0:
-            for part in gather_r:
-                part.wait(0)
-                part.start(1)
-        blocks(cot_groups, stage + 1)
     for part in gather_l:
-        part.wait(2)
+        part.wait(0)
+        part.start(1)
+    for part in gather_r:
+        part.wait(0)
+        part.start(1)
+    for name in ("in", "gate", "ker"):
+        loads[name].start()
+    blocks(cot_groups, 1)
+    blocks(cot_groups, 2)
+    for part in gather_l:
+        part.wait(1)
     swap_l.start()
     for part in gather_r:
         part.wait(1)
@@ -428,6 +522,7 @@
         back.arrived(j)
         twisted.start(j)
         push(j)
+
     save = [pltpu.make_async_copy(xker, gker_ref, stores.at[0])]
     save[0].start()
 
@@ -462,12 +557,12 @@
     pair_r = remote(sib_r, got_r, core_sems.at[0, 2], core_sems.at[1, 2], sibling)
     pair_r.start()
     reduce_r = [
-        Reduce(own_r, (d0_r, d1_r, d2_r), gright_ref, math.sqrt(A * C / H), *part, reduce_sems.at[0, 2 + n], reduce_sems.at[1, 2 + n])
+        Reduce(own_r, (d0_r, d1_r, d2_r), gright_ref, math.sqrt(A * C / H), *part, reduce_sems.at[0, n], reduce_sems.at[1, n])
         for n, part in enumerate(RIGHT_PARTS)
     ]
     reduce_l = [
-        Reduce(own_l, (d0_l, d1_l, d2_l), gleft_ref, math.sqrt(B * C / H), *part, reduce_sems.at[0, n], reduce_sems.at[1, n])
-        for n, part in enumerate(LEFT_PARTS)
+        PlaneReduce(own_l, (a0_l, a1_l), gleft_ref, math.sqrt(B * C / H), 0, True, axis_sems.at[2], plane_sems.at[2]),
+        PlaneReduce(own_l, (b0_l, b1_l), gleft_ref, math.sqrt(B * C / H), LANE, False, axis_sems.at[3], plane_sems.at[3]),
     ]
 
     def gated_dot(h, _):
@@ -547,7 +642,7 @@
 
         def body(i, row, lanes):
             for n, value in enumerate(from_groups(group_rows(j, row), masks)):
-                trecv[n, pl.ds(row, 16), lanes] = value.astype(BF)
+                out[(i // 16) * 8 + n, pl.ds(aligned((i % 16) * 16, 16), 16), lanes] = value.astype(BF)
 
         blocks(body, j)
 
@@ -555,11 +650,10 @@
         twisted.arrived(j)
         twist_groups(j)
         left_terms(j)
-        if j < 2:
+        if j == 1:
             for part in reduce_r:
-                part.finish(j)
-                part.start(j + 1)
-            outer(j)
+                part.finish(0)
+                part.start(1)
 
     def left_tile(seq, lo, which, lane):
         row = seq * 8 + lo * 4 + which * 2
@@ -585,22 +679,25 @@
     lax.fori_loop(0, SEQ, pack_left, 0)
     pair_l = remote(sib_l, got_l, core_sems.at[0, 3], core_sems.at[1, 3], sibling)
     pair_l.start()
-    for part in reduce_r:
-        part.finish(2)
+    outer(0)
     pair_l.wait()
     lax.fori_loop(0, SEQ, add_left, 0)
     for part in reduce_l:
         part.start(0)
+    for part in reduce_r:
+        part.finish(1)
+        part.start(2)
+    outer(1)
+    for part in reduce_l:
+        part.finish(0)
+        part.start(1)
     outer(2)
-    save.append(pltpu.make_async_copy(trecv.at[:, pl.ds(0, 256), :], out_ref.at[pl.ds(0, 8)], stores.at[3]))
-    save.append(pltpu.make_async_copy(trecv.at[:, pl.ds(256, 256), :], out_ref.at[pl.ds(8, 8)], stores.at[4]))
+    save.append(pltpu.make_async_copy(out, out_ref, stores.at[3]))
     save[3].start()
-    save[4].start()
-    for stage in range(3):
-        for part in reduce_l:
-            part.finish(stage)
-            if stage < 2:
-                part.start(stage + 1)
+    for part in reduce_r:
+        part.finish(2)
+    for part in reduce_l:
+        part.finish(1)
     for j in range(3):
         twisted.sent(j)
     for copy in save:
@@ -611,14 +708,6 @@
     hbm = pl.BlockSpec(memory_space=pl.ANY)
     vmem = pl.BlockSpec(memory_space=pltpu.VMEM)
     rows = pltpu.VMEM((8, B, 384), BF)
-
-    def heap(rows, lanes):
-        block = (rows, lanes)
-        return [pltpu.VMEM((4, 4, 4) + block, BF)] * 3 + [
-            pltpu.VMEM((3, 4, 4) + block, BF),
-            pltpu.VMEM((3, 4) + block, BF),
-            pltpu.VMEM((3,) + block, BF),
-        ]
 
     return pl.pallas_call(
         layer_kernel,
@@ -632,7 +721,8 @@
         ),
         in_specs=[hbm] * 6,
         out_specs=(hbm,) * 4 + (vmem,) * 2,
-        scratch_shapes=[rows] * 9
+        scratch_shapes=[pltpu.VMEM((16, A, 384), BF)]
+        + [rows] * 9
         + [
             pltpu.VMEM((H, B, B), BF),
             pltpu.VMEM((H, A, A), BF),
@@ -642,18 +732,25 @@
             pltpu.VMEM((4, 4, 4, 64, B), BF),
             pltpu.VMEM((4, 4, 4, 32, A), BF),
         ]
-        + heap(32, B)
-        + heap(16, A)
+        + [pltpu.VMEM((4, 4, 4, 32, B), BF)] * 3
+        + [pltpu.VMEM((3,) + (4,) * n + (32, B), BF) for n in (2, 1, 0)]
+        + [pltpu.VMEM((4, 4, 4, 16, A), BF)] * 3
         + [
+            pltpu.VMEM((3, 4, 4, 16, LANE), BF),
+            pltpu.VMEM((15, 16, LANE), BF),
+            pltpu.VMEM((15, 4, 16, LANE), BF),
+            pltpu.VMEM((3, 16, LANE), BF),
             pltpu.SemaphoreType.DMA((7,)),
             pltpu.SemaphoreType.DMA((2, 3)),
             pltpu.SemaphoreType.DMA((4, 3, SEQ)),
-            pltpu.SemaphoreType.DMA((5,)),
+            pltpu.SemaphoreType.DMA((4,)),
             pltpu.SemaphoreType.DMA((2, 4)),
-            pltpu.SemaphoreType.DMA((2, 5, 3, 3)),
-            pltpu.SemaphoreType.DMA((2, 5, 3, 3)),
+            pltpu.SemaphoreType.DMA((2, 3, 3, 3)),
+            pltpu.SemaphoreType.DMA((2, 3, 3, 3)),
+            pltpu.SemaphoreType.DMA((4, 2, 4)),
+            pltpu.SemaphoreType.DMA((4, 2, 16)),
         ],
-        compiler_params=pltpu.CompilerParams(collective_id=0, has_side_effects=True, vmem_limit_bytes=62 << 20),
+        compiler_params=pltpu.CompilerParams(collective_id=0, has_side_effects=True, vmem_limit_bytes=60 << 20),
         name="layer",
     )(inputs, gate_values, kernel, grad_out, right, left)
 

time: 188 us -> 178 us (0.947)
  Pallas kernels: 174 us -> 164 us
    pallas_call x1, Pallas kernels: 174 us -> 164 us  [layer(): pl.pallas_call(layer_kernel, out_shape=(jax.ShapeDtypeStruct((16, A, 384)...]
where the time goes in v3:
time: 178 us
  Pallas kernels  164 us (92%)
  local copies, waits for them, and re-layouts  13.1 us (7%)
    pallas_call x1, Pallas kernels, layer(): pl.pallas_call(layer_kernel, out_shape=(jax.ShapeDtypeStruct((16, A, 384)...  164 us
    unnamed x16, local copies, waits for them, and re-layouts  13.1 us

profile of v3, /device:TPU:0, one launch (start us, length us, event | category | flops | bytes accessed | tf_op | source)
XLA Modules:
  0.0 177.7 jit_solution(18162314307007897657)
XLA Ops:
  0.6 164.0 %layer.1 = (bf16[16,256,384]{2,1,0:T(8,128)(2,1)}, bf16[8,512,384]{2,1,0:T(8,128)(2,1)}, bf16[8,512,384]{2,1,0:T(8,128)(2,1)}, bf16[8,512,384]{2,1,0:T(8,128)(2,...) custom-call(bf16[8,512,384]{2,1,0:T(8,128)(2,1)} %in_ref.1, bf16[8,512,384]{2,1,0:T(8,128)(2,1)} %gate_ref.1, ...), custom_call_target="tpu_custom_call" | custom-call | tf_op jit(solution)/shard_map/layer/pallas_call | solution.py:712
  164.6 0.0 copy-start.2
  164.6 4.1 %copy.18 = bf16[16,256,384]{2,1,0:T(8,128)(2,1)} copy(bf16[16,256,384]{2,1,0:T(8,128)(2,1)} %get-tuple-element.24) | data formatting | bytes 6291456
  168.7 0.0 copy-done.2
  168.7 0.0 copy-start.1
  168.7 1.7 copy.19
  170.4 1.4 copy-done.1
  171.8 0.0 copy-start
  171.8 1.7 copy.20
  173.4 1.4 copy-done
  174.8 0.0 copy-start.4
  174.8 0.0 copy-start.3
  174.8 1.7 copy.21
  176.5 0.0 copy-done.4
  176.5 0.6 copy.22
  177.1 0.0 copy-done.3
  177.1 0.6 copy.23
Async XLA Ops:
  164.6 4.1 %copy-start.2 = (bf16[8,512,384]{2,1,0:T(8,128)(2,1)S(1)}, bf16[8,512,384]{2,1,0:T(8,128)(2,1)}, u32[]{:S(2)}) copy-start(bf16[8,512,384]{2,1,0:T(8,128)(2,1)} %get-tuple-element.25) | copy-start | bytes 9437188
  168.7 3.0 %copy-start.1 = (bf16[8,512,384]{2,1,0:T(8,128)(2,1)S(1)}, bf16[8,512,384]{2,1,0:T(8,128)(2,1)}, u32[]{:S(2)}) copy-start(bf16[8,512,384]{2,1,0:T(8,128)(2,1)} %get-tuple-element.26) | copy-start | bytes 9437188
  171.8 3.0 %copy-start = (bf16[8,512,384]{2,1,0:T(8,128)(2,1)S(1)}, bf16[8,512,384]{2,1,0:T(8,128)(2,1)}, u32[]{:S(2)}) copy-start(bf16[8,512,384]{2,1,0:T(8,128)(2,1)} %get-tuple-element.27) | copy-start | bytes 9437188
  174.8 1.7 copy-start.4
  174.8 2.3 %copy-start.3 = (f32[32,512]{1,0:T(8,128)S(1)}, f32[32,512]{1,0:T(8,128)}, u32[]{:S(2)}) copy-start(f32[32,512]{1,0:T(8,128)} %get-tuple-element.17) | copy-start | bytes 196612

commit v4 on v3

--- a/solution.py
+++ b/solution.py
@@ -17,7 +17,7 @@
 H = 8
 LANE = 128
 SEQ = 32
-RIGHT_PARTS = ((0, 256, (0, 1, 2)), (256, 128, (1, 2, 0)), (384, 128, (2, 0, 1)))
+RIGHT_PARTS = ((0, 16, 0, 384, (0, 1, 2)), (16, 16, 0, 384, (1, 2, 0)), (0, 32, 384, 128, (2, 0, 1)))
 
 
 def place():
@@ -135,14 +135,14 @@
 
 
 class Gather:
-    def __init__(self, buf, rows, lane, lanes, order, send, recv):
-        self.buf, self.rows, self.lanes, self.order = buf, rows, pl.ds(lane, lanes), order
+    def __init__(self, buf, row, rows, lane, lanes, order, send, recv):
+        self.buf, self.row, self.rows, self.lanes, self.order = buf, row, rows, pl.ds(lane, lanes), order
         self.send, self.recv = send, recv
 
     def copies(self, stage):
         xyz, core = place()
         index = tuple(slice(None) if axis in self.order[:stage] else xyz[axis] for axis in range(3))
-        ref = self.buf.at[index + (pl.ds(aligned(core * self.rows, self.rows), self.rows), self.lanes)]
+        ref = self.buf.at[index + (pl.ds(aligned(core * 32 + self.row, 16), self.rows), self.lanes)]
         return [
             remote(
                 ref,
@@ -164,9 +164,10 @@
 
 
 class Reduce:
-    def __init__(self, buf, heaps, out, scale, lane, lanes, order, send, recv):
+    def __init__(self, buf, heaps, out, scale, row, rows, lane, lanes, order, send, recv):
         self.buf, self.heaps, self.out, self.scale = buf, heaps, out, scale
-        self.lanes, self.order, self.send, self.recv = pl.ds(lane, lanes), order, send, recv
+        self.rows, self.lanes = pl.ds(row, rows), pl.ds(lane, lanes)
+        self.order, self.send, self.recv = order, send, recv
 
     def copies(self, stage):
         xyz, core = place()
@@ -177,8 +178,8 @@
             index = tuple(slice(None) if n in self.order[stage + 1 :] else to[n] for n in range(3))
             found.append(
                 remote(
-                    self.buf.at[index + (slice(None), self.lanes)],
-                    self.heaps[stage].at[(step - 1,) + (slice(None),) * (3 - stage) + (self.lanes,)],
+                    self.buf.at[index + (self.rows, self.lanes)],
+                    self.heaps[stage].at[(step - 1,) + (slice(None),) * (2 - stage) + (self.rows, self.lanes)],
                     self.send.at[stage, step - 1],
                     self.recv.at[stage, step - 1],
                     device_at(to, core),
@@ -201,12 +202,12 @@
             spots = [i // 4, i % 4][2 - len(rest) :]
             for axis, spot in zip(rest, spots):
                 at[axis] = spot
-            index = (*at, slice(None), self.lanes)
+            index = (*at, self.rows, self.lanes)
             value = self.buf[index].astype(F32)
             for step in range(3):
-                value = value + self.heaps[stage][(step, *spots, slice(None), self.lanes)].astype(F32)
+                value = value + self.heaps[stage][(step, *spots, self.rows, self.lanes)].astype(F32)
             if stage == 2:
-                self.out[:, self.lanes] = value / self.scale
+                self.out[self.rows, self.lanes] = value / self.scale
             else:
                 self.buf[index] = value.astype(BF)
             return carry
@@ -370,7 +371,7 @@
         PlaneGather(raw_l, LANE, False, axis_sems.at[1], plane_sems.at[1]),
     ]
     gather_r = [
-        Gather(raw_r, 32, *part, gather_sems.at[0, n], gather_sems.at[1, n])
+        Gather(raw_r, *part, gather_sems.at[0, n], gather_sems.at[1, n])
         for n, part in enumerate(RIGHT_PARTS)
     ]
     mine_l = raw_l.at[:, :, :, pl.ds(aligned(core * 16, 16), 16), :]
@@ -650,10 +651,6 @@
         twisted.arrived(j)
         twist_groups(j)
         left_terms(j)
-        if j == 1:
-            for part in reduce_r:
-                part.finish(0)
-                part.start(1)
 
     def left_tile(seq, lo, which, lane):
         row = seq * 8 + lo * 4 + which * 2
@@ -679,6 +676,9 @@
     lax.fori_loop(0, SEQ, pack_left, 0)
     pair_l = remote(sib_l, got_l, core_sems.at[0, 3], core_sems.at[1, 3], sibling)
     pair_l.start()
+    for part in reduce_r:
+        part.finish(0)
+        part.start(1)
     outer(0)
     pair_l.wait()
     lax.fori_loop(0, SEQ, add_left, 0)

time: 178 us -> 177 us (level)
  no operation moved by 1% of the time
where the time goes in v4:
time: 177 us
  Pallas kernels  163 us (92%)
  local copies, waits for them, and re-layouts  13.1 us (7%)
    pallas_call x1, Pallas kernels, layer(): pl.pallas_call(layer_kernel, out_shape=(jax.ShapeDtypeStruct((16, A, 384)...  163 us
    unnamed x16, local copies, waits for them, and re-layouts  13.1 us

profile of v4, /device:TPU:0, one launch (start us, length us, event | category | flops | bytes accessed | tf_op | source)
XLA Modules:
  0.0 176.6 jit_solution(3096083353472082304)
XLA Ops:
  0.6 162.8 %layer.1 = (bf16[16,256,384]{2,1,0:T(8,128)(2,1)}, bf16[8,512,384]{2,1,0:T(8,128)(2,1)}, bf16[8,512,384]{2,1,0:T(8,128)(2,1)}, bf16[8,512,384]{2,1,0:T(8,128)(2,...) custom-call(bf16[8,512,384]{2,1,0:T(8,128)(2,1)} %in_ref.1, bf16[8,512,384]{2,1,0:T(8,128)(2,1)} %gate_ref.1, ...), custom_call_target="tpu_custom_call" | custom-call | tf_op jit(solution)/shard_map/layer/pallas_call | solution.py:712
  163.5 0.0 copy-start.2
  163.5 4.1 %copy.18 = bf16[16,256,384]{2,1,0:T(8,128)(2,1)} copy(bf16[16,256,384]{2,1,0:T(8,128)(2,1)} %get-tuple-element.24) | data formatting | bytes 6291456
  167.6 0.0 copy-done.2
  167.6 0.0 copy-start.1
  167.6 1.7 copy.19
  169.3 1.4 copy-done.1
  170.6 0.0 copy-start
  170.6 1.7 copy.20
  172.3 1.4 copy-done
  173.7 0.0 copy-start.4
  173.7 0.0 copy-start.3
  173.7 1.7 copy.21
  175.3 0.0 copy-done.4
  175.3 0.6 copy.22
  175.9 0.0 copy-done.3
  175.9 0.6 copy.23
Async XLA Ops:
  163.5 4.1 %copy-start.2 = (bf16[8,512,384]{2,1,0:T(8,128)(2,1)S(1)}, bf16[8,512,384]{2,1,0:T(8,128)(2,1)}, u32[]{:S(2)}) copy-start(bf16[8,512,384]{2,1,0:T(8,128)(2,1)} %get-tuple-element.25) | copy-start | bytes 9437188
  167.6 3.0 %copy-start.1 = (bf16[8,512,384]{2,1,0:T(8,128)(2,1)S(1)}, bf16[8,512,384]{2,1,0:T(8,128)(2,1)}, u32[]{:S(2)}) copy-start(bf16[8,512,384]{2,1,0:T(8,128)(2,1)} %get-tuple-element.26) | copy-start | bytes 9437188
  170.6 3.0 %copy-start = (bf16[8,512,384]{2,1,0:T(8,128)(2,1)S(1)}, bf16[8,512,384]{2,1,0:T(8,128)(2,1)}, u32[]{:S(2)}) copy-start(bf16[8,512,384]{2,1,0:T(8,128)(2,1)} %get-tuple-element.27) | copy-start | bytes 9437188
  173.7 1.7 copy-start.4
  173.7 2.3 %copy-start.3 = (f32[32,512]{1,0:T(8,128)S(1)}, f32[32,512]{1,0:T(8,128)}, u32[]{:S(2)}) copy-start(f32[32,512]{1,0:T(8,128)} %get-tuple-element.17) | copy-start | bytes 196612
